TPU v7x, 32 devices: a whole 2x2x4 slice. The times are simulated.
32 devices in a mesh: blk: 4 (over y, x), dp: 8 (over z, core).
Axes of the slice: x: 2, y: 2, z: 4, core: 2. Of those that a mesh axis runs over, the one named last changes fastest.
Arguments:
- queries: bfloat16 [4096, 4096], P(('blk', 'dp')), may hold values from -6 to 6
- passages: bfloat16 [4096, 4096], P(('blk', 'dp')), may hold values from -6 to 6
- hard_ids: int32 [4096, 8], P(('blk', 'dp')), may hold values from 0 to 1023, as said below
- query_weight: float32 [4096], P(('blk', 'dp')), may hold values from 4 to 40
Outputs:
- query_grads: float32 [4096, 4096], P(('blk', 'dp'))
- passage_grads: float32 [4096, 4096], P(('blk', 'dp'))
- mean_loss: float32 [], replicated
Inputs may be any that keep to these rules, and one draw needn't show every extreme that they name: `hard_ids`: of the 1024 ids of one device's queries, at most 192 have the same value of id // 128, and in every device's block some value has exactly 192.
All inputs are finite; a program needn't handle non-finite values.
Results may differ from a plain program's by a relative error of at most 0.0034.
Values may be sent and summed in bfloat16 or wider, within the bound.
A program may use at most 192 MiB of HBM per device.

v0:
```python
import math

import jax
import jax.numpy as jnp
from jax import lax
from jax.sharding import PartitionSpec as P


def local(queries, passages, hard_ids, query_weight):
    rows_dev = queries.shape[0]
    width = queries.shape[1]
    hard_count = hard_ids.shape[1]
    rescale = 4.0 / math.sqrt(width)
    blk_count = lax.axis_size("blk")
    dp_count = lax.axis_size("dp")
    capacity = 12 * rows_dev // dp_count
    blk_index = lax.axis_index("blk")
    local_rows = jnp.arange(rows_dev, dtype=jnp.int32)
    group_rows = lax.all_gather(passages, "blk", axis=0, tiled=True)
    logits = (
        jnp.einsum("rd,pd->rp", queries, group_rows, preferred_element_type=jnp.float32) * rescale
    )
    flat_ids = hard_ids.reshape(-1)
    owner_dev = flat_ids // rows_dev
    row_local = flat_ids % rows_dev
    owner_hot = (owner_dev[:, None] == jnp.arange(dp_count, dtype=jnp.int32)[None, :]).astype(
        jnp.int32
    )
    slot_rank = jnp.sum((jnp.cumsum(owner_hot, axis=0) - 1) * owner_hot, axis=1)
    send_rows = jnp.zeros((dp_count, capacity), jnp.int32).at[owner_dev, slot_rank].set(row_local)
    wanted = lax.all_to_all(send_rows, "dp", split_axis=0, concat_axis=0, tiled=True)
    served = passages[wanted]
    arrived = lax.all_to_all(served, "dp", split_axis=0, concat_axis=0, tiled=True)
    negatives = arrived[owner_dev, slot_rank].reshape(rows_dev, hard_count, width)
    hard_logits = (
        jnp.einsum("rd,rkd->rk", queries, negatives, preferred_element_type=jnp.float32) * rescale
    )
    highest = jnp.maximum(jnp.max(logits, axis=1), jnp.max(hard_logits, axis=1))
    sumexp = jnp.sum(jnp.exp(logits - highest[:, None]), axis=1) + jnp.sum(
        jnp.exp(hard_logits - highest[:, None]), axis=1
    )
    lse = highest + jnp.log(sumexp)
    own_block = lax.dynamic_slice_in_dim(logits, blk_index * rows_dev, rows_dev, 1)
    positive = jnp.diagonal(own_block)
    loss_part = jnp.sum(query_weight * (lse - positive))
    mean_loss = lax.psum(loss_part, ("blk", "dp")) / (rows_dev * blk_count * dp_count)
    coefs = rescale * query_weight
    tile_cols = jnp.arange(blk_count * rows_dev, dtype=jnp.int32)
    own_cols = blk_index * rows_dev + local_rows
    positive_mask = (tile_cols[None, :] == own_cols[:, None]).astype(jnp.float32)
    tile_coef = (coefs[:, None] * (jnp.exp(logits - lse[:, None]) - positive_mask)).astype(
        jnp.bfloat16
    )
    hard_coef = (coefs[:, None] * jnp.exp(hard_logits - lse[:, None])).astype(jnp.bfloat16)
    query_grads = jnp.dot(tile_coef, group_rows, preferred_element_type=jnp.float32)
    query_grads = query_grads + jnp.einsum(
        "rk,rkd->rd", hard_coef, negatives, preferred_element_type=jnp.float32
    )
    hard_terms = (hard_coef[:, :, None] * queries[:, None, :]).reshape(-1, width)
    slots = (
        jnp.zeros((dp_count, capacity, width), jnp.bfloat16)
        .at[owner_dev, slot_rank]
        .set(hard_terms)
    )
    returned = lax.all_to_all(slots, "dp", split_axis=0, concat_axis=0, tiled=True)
    selector = (wanted.reshape(-1)[None, :] == local_rows[:, None]).astype(jnp.bfloat16)
    hard_grads = jnp.dot(selector, returned.reshape(-1, width), preferred_element_type=jnp.float32)
    tile_grads = lax.psum_scatter(
        jnp.einsum("rp,rd->pd", tile_coef, queries, preferred_element_type=jnp.float32),
        "blk",
        scatter_dimension=0,
        tiled=True,
    )
    passage_grads = tile_grads + hard_grads
    return (query_grads, passage_grads, mean_loss)


def solution(mesh):
    return jax.shard_map(
        local,
        mesh=mesh,
        in_specs=(
            P(("blk", "dp"), None),
            P(("blk", "dp"), None),
            P(("blk", "dp"), None),
            P(("blk", "dp")),
        ),
        out_specs=(P(("blk", "dp"), None), P(("blk", "dp"), None), P()),
        check_vma=False,
    )
```

profile of v0, /device:TPU:0, one launch (start us, length us, event | category | flops | bytes accessed | tf_op | source)
XLA Modules:
  0.0 726.2 jit_solution(4558662524227886952)
XLA Ops:
  7.2 0.8 copy.7
  8.0 0.1 reshape.203
  8.0 0.1 reshape.202
  8.1 0.1 reshape.201
  8.3 2.3 reduce-window.6
  10.5 0.3 slice_reduce_fusion
  10.8 0.2 reduce-window.9
  11.0 0.1 add_bitcast_fusion
  11.2 0.7 and_reduce_fusion
  11.9 0.7 multiply_reduce_fusion.1
  12.7 4.3 scatter_custom_fusion
  17.0 0.1 all_to_all.14
  17.1 11.7 %all_to_all.22 = s32[8,1,192]{2,1,0:T(1,128)S(1)} all-to-all(s32[8,1,192]{2,1,0:T(1,128)S(1)} %all_to_all.14), channel_id=1, replica_groups=mesh['blk'=4,'dp'=8] {'dp'}, dimensions={0} | all-to-all | bytes 12288 | tf_op jit(solution)/shard_map/all_to_all | solution.py:31
  28.8 0.1 reshape.218
  28.9 23.4 %gather_fusion = bf16[1536,4096]{1,0:T(8,128)(2,1)} fusion(bf16[128,4096]{1,0:T(8,128)(2,1)} %param.5, s32[2048]{0:T(1024)S(1)} %pad_clamp_fusion), kind=kCustom, calls=%fused_computation | custom fusion | bytes 25171968 | tf_op jit(solution)/shard_map/gather | solution.py:32
  52.3 0.0 copy-start.1
  52.3 5.5 all-to-all-start.1
  57.8 0.2 all-gather.2.cloned.1.call-start
  58.1 0.5 all-gather.2.cloned.1.call-update
  58.6 56.0 %all-gather.2.cloned.1.call-done = bf16[512,4096]{1,0:T(8,128)(2,1)} async-done(((bf16[128,4096]{1,0:T(8,128)(2,1)}), bf16[512,4096]{1,0:T(8,128)(2,1)}) %all-gather.2.cloned.1.call-update) | async-done | bytes 4194320 | tf_op jit(solution)/shard_map/all_gather | solution.py:19
  114.6 0.0 copy-done.1
  114.6 3.8 fusion.20
  118.4 1.2 gather_fusion.2
  119.7 211.9 %all-to-all-done.1 = bf16[8,192,4096]{2,1,0:T(8,128)(2,1)} async-done(((bf16[8,192,4096]{2,1,0:T(8,128)(2,1)}), bf16[8,192,4096]{2,1,0:T(8,128)(2,1)}, u32[]{:S(2)}, u32[]{:S(2)}) %all-to-all-start.1) | async-done | bytes 12582944 | tf_op jit(solution)/shard_map/all_to_all | solution.py:33
  331.6 34.4 %gather_fusion.1 = bf16[1024,4096]{1,0:T(8,128)(2,1)} fusion(bf16[8,192,4096]{2,1,0:T(8,128)(2,1)} %all-to-all-done.1, s32[1024]{0:T(1024)S(1)} %bitcast.43), kind=kCustom, calls=%fused_computation.1 | custom fusion | bytes 16785408 | tf_op jit(solution)/shard_map/gather | solution.py:34
  366.0 0.0 copy-start.2
  366.0 8.9 %fusion.2 = f32[128,1,8]{2,1,0:T(1,128)S(1)} fusion(bf16[1024,4096]{1,0:T(8,128)(2,1)} %gather_fusion.1, bf16[128,4096,1]{1,0,2:T(8,128)(2,1)S(1)} %bitcast.46), kind=kOutput, calls=%fused_computation.8 | convolution fusion | flops 8388608 | bytes 9441280 | tf_op jit(solution)/shard_map/rd,rkd->rk/dot_general | solution.py:36
  374.8 0.1 multiply_reduce_fusion
  375.0 0.2 exponential_reduce_fusion
  375.2 0.2 exponential_reduce_fusion.1
  375.3 0.0 copy-done.2
  375.4 0.6 multiply_reduce_fusion.2
  376.0 0.1 multiply_convert_fusion.1
  376.1 0.1 mul.74
  376.2 4.3 bitcast_multiply_fusion
  380.5 20.1 %scatter_custom_fusion.1 = bf16[1536,4096]{1,0:T(8,128)(2,1)} fusion(s32[1024]{0:T(1024)S(1)} %broadcast_select_fusion, bf16[1024,4096]{1,0:T(8,128)(2,1)} %bitcast_multiply_fusion, bf16[]{:T(256)} %constant.64.clone.1), kind=kCustom, calls=%fused_computation.10 | custom fusion | bytes 12583424
  400.6 5.4 all-to-all-start.2
  406.0 0.0 reduce-scatter.2.cloned.1.call-start
  406.1 4.6 fusion.19
  410.6 0.0 reduce-scatter.2.cloned.1.call-update
  410.7 0.1 eq.60
  410.8 289.2 %psum.7 = f32[]{:T(128)} all-reduce(f32[]{:T(128)} %get-tuple-element.3), channel_id=1, replica_groups=mesh['blk'=4,'dp'=8] {'blk','dp'}, use_global_device_ids=true, to_apply=%region_11.12 | all-reduce | flops 1 | bytes 8 | tf_op jit(solution)/shard_map/psum | solution.py:46
  700.6 0.0 copy-start
  700.7 0.1 fusion.26
  700.8 5.9 fusion
  706.6 0.0 copy-done
  706.6 3.3 convolution_add_fusion
  709.9 0.0 reduce-scatter.2.cloned.1.call-done
  709.9 0.0 all-to-all-done.2
  710.0 8.3 %convolution_add_fusion.1 = f32[128,4096]{1,0:T(8,128)} fusion(f32[128,4096]{1,0:T(8,128)} %reduce-scatter.2.cloned.1.call-done, bf16[1536,4096]{1,0:T(8,128)(2,1)} %bitcast.13, s32[1536]{0:T(1024)S(1)} %eq.60), kind=kOutput, calls=%fused_computation.13 | convolution fusion | flops 1611333632 | bytes 16783360 | tf_op jit(solution)/shard_map/dot_general | solution.py:67
  (13 shorter events, 0.2 us)
Async XLA Ops:
  52.3 62.3 %copy-start.1 = (bf16[128,4096]{1,0:T(8,128)(2,1)S(1)}, bf16[128,4096]{1,0:T(8,128)(2,1)}, u32[]{:S(2)}) copy-start(bf16[128,4096]{1,0:T(8,128)(2,1)} %param.4) | copy-start | bytes 3145732
  52.3 279.3 %all-to-all-start.1 = ((bf16[8,192,4096]{2,1,0:T(8,128)(2,1)}), bf16[8,192,4096]{2,1,0:T(8,128)(2,1)}, u32[]{:S(2)}, u32[]{:S(2)}) async-start(bf16[8,192,4096]{2,1,0:T(8,128)(2,1)} %bitcast.44), calls=%async_computation.1 | async-start | bytes 25165824 | tf_op jit(solution)/shard_map/all_to_all | solution.py:33
  57.8 56.8 %all-gather.2.cloned.1.call-start = ((), (), s32[]{:S(2)}) async-start(), calls=%async_computation.4 | async-start | bytes 5242880 | tf_op jit(solution)/shard_map/all_gather | solution.py:19
  366.0 9.4 %copy-start.2 = (f32[128]{0:T(128)S(1)}, f32[128]{0:T(128)}, u32[]{:S(2)}) copy-start(f32[128]{0:T(128)} %param.7) | copy-start | bytes 1540
  400.6 309.4 %all-to-all-start.2 = ((bf16[8,192,4096]{2,1,0:T(8,128)(2,1)}), bf16[8,192,4096]{2,1,0:T(8,128)(2,1)}, u32[]{:S(2)}, u32[]{:S(2)}) async-start(bf16[8,192,4096]{2,1,0:T(8,128)(2,1)} %bitcast.45), calls=%async_computation.3 | async-start | bytes 25165824 | tf_op jit(solution)/shard_map/all_to_all | solution.py:65
  406.0 304.0 %reduce-scatter.2.cloned.1.call-start = ((), (), s32[]{:S(2)}) async-start(), calls=%async_computation.5 | async-start | bytes 10485760 | tf_op jit(solution)/shard_map/reduce_scatter | solution.py:68
  700.6 6.0 copy-start
Sparse Core Ops, SparseCore 0:
  60.5 54.0 all-gather.1
  410.8 88.0 reduce-scatter.1
where the time goes:
time: 727 us; the launch traced here: 726 us
  blocking collectives  301 us (41%)
  waiting for transfers between devices  268 us (37%)
  local copies, waits for them, and re-layouts  85.2 us (12%)
  matrix products  34.8 us (5%)
  between operations  16 us (2%)
  starting transfers between devices  11.1 us (2%)
  other arithmetic  9.8 us (1%)
    psum x1, blocking collectives, local(): lax.psum(loss_part, ('blk', 'dp')) / (rows_dev * blk_count * dp_count)  289 us
    all_to_all x1, waiting for transfers between devices, local(): lax.all_to_all(served, 'dp', split_axis=0, concat_axis=0, tiled=True)  212 us
    all_gather x1, waiting for transfers between devices, local(): group_rows = lax.all_gather(passages, 'blk', axis=0, tiled=True)  56 us
    gather x1, local copies, waits for them, and re-layouts, local(): arrived[owner_dev, slot_rank].reshape(rows_dev, hard_count, width)  34.4 us
    unnamed x9, local copies, waits for them, and re-layouts  25.2 us
    gather x1, local copies, waits for them, and re-layouts, local(): served = passages[wanted]  23.4 us
  transfers between devices with their start and end apart: 4, of which 2 were waited for; matrix products, arithmetic and copies ran while one was open for 3% of the time, Pallas kernels for 0%

commit v1 on v0

v1 whole, which is shorter than its diff:
```python
import math

import jax
import jax.numpy as jnp
from jax import lax
from jax.sharding import PartitionSpec as P


def pooled(queries, passages, hard_ids, query_weight):
    rows_dev = queries.shape[0]
    width = queries.shape[1]
    hard_count = hard_ids.shape[1]
    rescale = 4.0 / math.sqrt(width)
    blk_count = lax.axis_size("blk")
    dp_count = lax.axis_size("dp")
    blk_index = lax.axis_index("blk")
    local_rows = jnp.arange(rows_dev, dtype=jnp.int32)
    pool_passages = lax.all_gather(passages, "dp", axis=0, tiled=True)
    group_passages = lax.all_gather(passages, "blk", axis=0, tiled=True)
    pool_queries = lax.all_gather(queries, "dp", axis=0, tiled=True)
    group_queries = lax.all_gather(queries, "blk", axis=0, tiled=True)
    contract = (((1,), (1,)), ((), ()))
    tile = lax.dot_general(queries, group_passages, contract, preferred_element_type=jnp.float32)
    tile = tile * rescale
    pool = lax.dot_general(queries, pool_passages, contract, preferred_element_type=jnp.float32)
    pool = pool * rescale
    pool_cols = jnp.arange(dp_count * rows_dev, dtype=jnp.int32)
    times = jnp.zeros(pool.shape, jnp.float32)
    for k in range(hard_count):
        times = times + (hard_ids[:, k : k + 1] == pool_cols[None, :]).astype(jnp.float32)
    taken = jnp.where(times > 0.0, pool, -jnp.inf)
    highest = jnp.maximum(jnp.max(tile, axis=1), jnp.max(taken, axis=1))
    sumexp = jnp.sum(jnp.exp(tile - highest[:, None]), axis=1) + jnp.sum(
        times * jnp.exp(taken - highest[:, None]), axis=1
    )
    lse = highest + jnp.log(sumexp)
    tile_cols = jnp.arange(blk_count * rows_dev, dtype=jnp.int32)
    own = tile_cols[None, :] == (blk_index * rows_dev + local_rows)[:, None]
    positive = jnp.sum(jnp.where(own, tile, 0.0), axis=1)
    loss_part = jnp.sum(query_weight * (lse - positive))
    mean_loss = lax.psum(loss_part, ("blk", "dp")) / (rows_dev * blk_count * dp_count)
    coefs = (rescale * query_weight)[:, None]
    tile_coef = (coefs * (jnp.exp(tile - lse[:, None]) - own.astype(jnp.float32))).astype(
        jnp.bfloat16
    )
    one_coef = (coefs * jnp.exp(taken - lse[:, None])).astype(jnp.bfloat16)
    pool_coef = (times * one_coef.astype(jnp.float32)).astype(jnp.bfloat16)
    query_grads = jnp.dot(tile_coef, group_passages, preferred_element_type=jnp.float32) + jnp.dot(
        pool_coef, pool_passages, preferred_element_type=jnp.float32
    )
    back_tile = lax.all_to_all(
        tile_coef.T.reshape(blk_count, rows_dev, rows_dev), "blk", 0, 0, tiled=True
    )
    back_pool = lax.all_to_all(
        pool_coef.T.reshape(dp_count, rows_dev, rows_dev), "dp", 0, 0, tiled=True
    )
    back_tile = back_tile.transpose(1, 0, 2).reshape(rows_dev, -1)
    back_pool = back_pool.transpose(1, 0, 2).reshape(rows_dev, -1)
    passage_grads = jnp.dot(back_tile, group_queries, preferred_element_type=jnp.float32) + jnp.dot(
        back_pool, pool_queries, preferred_element_type=jnp.float32
    )
    return (query_grads, passage_grads, mean_loss)


def solution(mesh):
    return jax.shard_map(
        pooled,
        mesh=mesh,
        in_specs=(
            P(("blk", "dp"), None),
            P(("blk", "dp"), None),
            P(("blk", "dp"), None),
            P(("blk", "dp")),
        ),
        out_specs=(P(("blk", "dp"), None), P(("blk", "dp"), None), P()),
        check_vma=False,
    )
```

time: 727 us -> 303 us (0.42)
  blocking collectives: 301 us -> 44.1 us
  local copies, waits for them, and re-layouts: 85.2 us -> 0.02 us
  waiting for transfers between devices: 268 us -> 202 us
    psum x1, blocking collectives: 289 us -> 44.1 us  [pooled(): lax.psum(loss_part, ('blk', 'dp')) / (rows_dev * blk_count * dp_count)]
    all_to_all x2, waiting for transfers between devices: 212 us -> 0.01 us  [the longest x1 0.01 us: pooled(): lax.all_to_all(pool_coef.T.reshape(dp_count, rows_dev, rows_dev), 'dp', 0...]
    all_gather x1 -> x4, waiting for transfers between devices: 56 us -> 200 us  [the longest x1 79.9 us: pooled(): pool_passages = lax.all_gather(passages, 'dp', axis=0, tiled=True)]
    gather x3 -> x0, local copies, waits for them, and re-layouts: 59.1 us -> none  [the longest x1 34.4 us: local(): arrived[owner_dev, slot_rank].reshape(rows_dev, hard_count, width)]
    unnamed x9 -> x8, local copies, waits for them, and re-layouts: 25.2 us -> 0.02 us
    all_to_all x1 -> x0, blocking collectives: 11.7 us -> none  [local(): lax.all_to_all(send_rows, 'dp', split_axis=0, concat_axis=0, tiled=True)]
  transfers between devices with their start and end apart: 4 -> 6, of which waited for: 2 -> 4; matrix products, arithmetic and copies ran while one was open for 3% -> 10% of each run, Pallas kernels for 0% -> 0%
where the time goes in v1:
time: 303 us
  waiting for transfers between devices  202 us (67%)
  blocking collectives  44.1 us (15%)
  matrix products  29.2 us (10%)
  between operations  15.6 us (5%)
  starting transfers between devices  7.3 us (2%)
  other arithmetic  3.96 us (1%)
    all_gather x1, waiting for transfers between devices, pooled(): pool_passages = lax.all_gather(passages, 'dp', axis=0, tiled=True)  79.9 us
    all_gather x1, waiting for transfers between devices, pooled(): group_passages = lax.all_gather(passages, 'blk', axis=0, tiled=True)  55.3 us
    all_gather x1, waiting for transfers between devices, pooled(): group_queries = lax.all_gather(queries, 'blk', axis=0, tiled=True)  48.2 us
    psum x1, blocking collectives, pooled(): lax.psum(loss_part, ('blk', 'dp')) / (rows_dev * blk_count * dp_count)  44.1 us
    all_gather x1, waiting for transfers between devices, pooled(): pool_queries = lax.all_gather(queries, 'dp', axis=0, tiled=True)  16.3 us
    dot_general x1, matrix products, pooled(): lax.dot_general(queries, pool_passages, contract, preferred_element_type=...  6.67 us
  transfers between devices with their start and end apart: 6, of which 4 were waited for; matrix products, arithmetic and copies ran while one was open for 10% of the time, Pallas kernels for 0%

profile of v1, /device:TPU:0, one launch (start us, length us, event | category | flops | bytes accessed | tf_op | source)
XLA Modules:
  0.0 302.6 jit_solution(3239391073556734281)
XLA Ops:
  7.2 0.0 copy-start
  7.2 0.0 copy-start.2
  7.2 0.0 all-gather.5.cloned.1.call-start
  7.2 0.7 all-gather.5.cloned.1.call-update
  7.9 0.0 all-gather.7.cloned.1.call-start
  8.0 0.7 all-gather.7.cloned.1.call-update
  8.7 0.0 all-gather.11.cloned.1.call-start
  8.7 0.7 all-gather.11.cloned.1.call-update
  9.4 0.0 all-gather.9.cloned.1.call-start
  9.4 0.5 all-gather.9.cloned.1.call-update
  10.0 0.0 copy-done.2
  10.0 55.3 %all-gather.5.cloned.1.call-done = bf16[512,4096]{1,0:T(8,128)(2,1)} async-done(((bf16[128,4096]{1,0:T(8,128)(2,1)}), bf16[512,4096]{1,0:T(8,128)(2,1)}) %all-gather.5.cloned.1.call-update) | async-done | bytes 4194320 | tf_op jit(solution)/shard_map/all_gather | solution.py:19
  65.3 0.0 copy-done
  65.3 3.8 %fusion.18 = (f32[128]{0:T(128)S(1)}, f32[128,512]{1,0:T(8,128)S(1)}) fusion(bf16[128,4096]{1,0:T(8,128)(2,1)S(1)} %copy-done, bf16[512,4096]{1,0:T(8,128)(2,1)} %all-gather.5.cloned.1.call-done), kind=kOutput, calls=%fused_computation.67 | convolution fusion | flops 537001856 | bytes 5505536 | tf_op jit(solution)/shard_map/dot_general | solution.py:23
  69.1 79.9 %all-gather.7.cloned.1.call-done = bf16[1024,4096]{1,0:T(8,128)(2,1)} async-done(((bf16[128,4096]{1,0:T(8,128)(2,1)}), bf16[1024,4096]{1,0:T(8,128)(2,1)}) %all-gather.7.cloned.1.call-update) | async-done | bytes 8388624 | tf_op jit(solution)/shard_map/all_gather | solution.py:18
  149.0 0.0 copy-start.3
  149.0 6.7 %fusion.9 = (f32[128]{0:T(128)S(1)}, f32[128,1024]{1,0:T(8,128)S(1)}) fusion(s32[128]{0:T(128)S(1)} %get-tuple-element.13, s32[128]{0:T(128)S(1)} %get-tuple-element.14, s32[128]{0:T(128)S(1)} %get-tuple-element.8, s32[128]{0:T(128)S(1)} %get-tuple-element.9, s32[128]{0:T(128)S(1)} %get-tuple-element.10, s32[128]{0:T(128)S(1)} %get-tuple-element.11, ...), kind=kOutput, calls=%fused_computation.45 | convolution fusion | flops 1077280640 | bytes 9966080 | tf_op jit(solution)/shard_map/dot_general | solution.py:25
  155.7 0.0 copy-start.1
  155.7 0.2 select_reduce_fusion
  155.9 0.9 multiply_reduce_fusion
  156.9 0.0 copy-done.3
  156.9 0.6 multiply_reduce_fusion.1
  157.5 0.0 copy-done.1
  157.5 1.4 copy_bitcast_fusion
  158.8 3.4 %all-to-all-start.1 = ((bf16[8,128,128]{1,2,0:T(8,128)(2,1)}), bf16[8,128,128]{1,2,0:T(8,128)(2,1)S(1)}, u32[]{:S(2)}, u32[]{:S(2)}) async-start(bf16[8,128,128]{1,2,0:T(8,128)(2,1)} %copy_bitcast_fusion), calls=%async_computation.1 | async-start | bytes 524288 | tf_op jit(solution)/shard_map/all_to_all | solution.py:54
  162.3 5.5 %fusion.4 = f32[128,4096]{1,0:T(8,128)S(1)} fusion(bf16[1024,4096]{1,0:T(8,128)(2,1)} %all-gather.7.cloned.1.call-done, f32[128]{0:T(128)S(1)} %get-tuple-element.6, f32[128]{0:T(128)S(1)} %get-tuple-element.15, f32[128,1024]{1,0:T(8,128)} %copy-done.1, s32[128]{0:T(128)S(1)} %get-tuple-element.13, s32[128]{0:T(128)S(1)} %get-tuple-element.14, ...), kind=kOutput, calls=%fused_computation.32 | convolution fusion | flops 1077805056 | bytes 11015168 | tf_op jit(solution)/shard_map/dot_general | solution.py:48
  167.8 0.8 copy_bitcast_fusion.1
  168.6 44.1 %psum.7 = f32[]{:T(128)} all-reduce(f32[]{:T(128)} %get-tuple-element.5), channel_id=1, replica_groups=mesh['blk'=4,'dp'=8] {'blk','dp'}, use_global_device_ids=true, to_apply=%region_6.7 | all-reduce | flops 1 | bytes 8 | tf_op jit(solution)/shard_map/psum | solution.py:41
  213.4 4.3 %convolution_add_fusion.1 = f32[128,4096]{1,0:T(8,128)} fusion(f32[128,4096]{1,0:T(8,128)S(1)} %fusion.4, bf16[512,4096]{1,0:T(8,128)(2,1)} %all-gather.5.cloned.1.call-done, f32[128,512]{1,0:T(8,128)S(1)} %get-tuple-element.17, s32[128]{0:T(128)S(1)} %iota_add_fusion, f32[128]{0:T(128)S(1)} %get-tuple-element.6, f32[128]{0:T(128)S(1)} %get-tuple-element.15), kind=kOutput, calls=%fused_computation.1 | convolution fusion | flops 537788416 | bytes 8652288 | tf_op jit(solution)/shard_map/dot_general | solution.py:48
  217.7 0.0 all-to-all-done.1
  217.7 3.7 %all-to-all-start = ((bf16[4,128,128]{1,2,0:T(8,128)(2,1)}), bf16[4,128,128]{1,2,0:T(8,128)(2,1)S(1)}, u32[]{:S(2)}, u32[]{:S(2)}) async-start(bf16[4,128,128]{1,2,0:T(8,128)(2,1)} %copy_bitcast_fusion.1), calls=%async_computation | async-start | bytes 262144 | tf_op jit(solution)/shard_map/all_to_all | solution.py:51
  221.5 16.3 %all-gather.11.cloned.1.call-done = bf16[1024,4096]{1,0:T(8,128)(2,1)} async-done(((bf16[128,4096]{1,0:T(8,128)(2,1)}), bf16[1024,4096]{1,0:T(8,128)(2,1)}) %all-gather.11.cloned.1.call-update) | async-done | bytes 8388624 | tf_op jit(solution)/shard_map/all_gather | solution.py:20
  237.8 4.7 %fusion.19 = f32[128,4096]{1,0:T(8,128)S(1)} fusion(bf16[128,1024]{0,1:T(8,128)(2,1)S(1)} %bitcast.66, bf16[1024,4096]{1,0:T(8,128)(2,1)} %all-gather.11.cloned.1.call-done), kind=kOutput, calls=%fused_computation.68 | convolution fusion | flops 1073741824 | bytes 10747904 | tf_op jit(solution)/shard_map/dot_general | solution.py:59
  242.5 48.2 %all-gather.9.cloned.1.call-done = bf16[512,4096]{1,0:T(8,128)(2,1)} async-done(((bf16[128,4096]{1,0:T(8,128)(2,1)}), bf16[512,4096]{1,0:T(8,128)(2,1)}) %all-gather.9.cloned.1.call-update) | async-done | bytes 4194320 | tf_op jit(solution)/shard_map/all_gather | solution.py:21
  290.7 0.0 all-to-all-done
  290.7 4.3 %convolution_add_fusion = f32[128,4096]{1,0:T(8,128)} fusion(f32[128,4096]{1,0:T(8,128)S(1)} %fusion.19, bf16[128,512]{0,1:T(8,128)(2,1)S(1)} %bitcast.67, bf16[512,4096]{1,0:T(8,128)(2,1)} %all-gather.9.cloned.1.call-done), kind=kOutput, calls=%fused_computation | convolution fusion | flops 537395200 | bytes 8519680 | tf_op jit(solution)/shard_map/dot_general | solution.py:59
  (3 shorter events, 0.0 us)
Async XLA Ops:
  7.2 58.1 %copy-start = (bf16[128,4096]{1,0:T(8,128)(2,1)S(1)}, bf16[128,4096]{1,0:T(8,128)(2,1)}, u32[]{:S(2)}) copy-start(bf16[128,4096]{1,0:T(8,128)(2,1)} %param.4) | copy-start | bytes 3145732
  7.2 2.8 copy-start.2
  7.2 58.1 %all-gather.5.cloned.1.call-start = ((), (), s32[]{:S(2)}) async-start(), calls=%async_computation.2 | async-start | bytes 5242880 | tf_op jit(solution)/shard_map/all_gather | solution.py:19
  7.9 141.1 %all-gather.7.cloned.1.call-start = ((), (), s32[]{:S(2)}) async-start(), calls=%async_computation.3 | async-start | bytes 9437184 | tf_op jit(solution)/shard_map/all_gather | solution.py:18
  8.7 229.1 %all-gather.11.cloned.1.call-start = ((), (), s32[]{:S(2)}) async-start(), calls=%async_computation.5 | async-start | bytes 9437184 | tf_op jit(solution)/shard_map/all_gather | solution.py:20
  9.4 281.3 %all-gather.9.cloned.1.call-start = ((), (), s32[]{:S(2)}) async-start(), calls=%async_computation.4 | async-start | bytes 5242880 | tf_op jit(solution)/shard_map/all_gather | solution.py:21
  149.0 7.9 %copy-start.3 = (f32[128]{0:T(128)S(1)}, f32[128]{0:T(128)}, u32[]{:S(2)}) copy-start(f32[128]{0:T(128)} %param.7) | copy-start | bytes 1540
  155.7 1.8 copy-start.1
  158.8 58.9 %all-to-all-start.1 = ((bf16[8,128,128]{1,2,0:T(8,128)(2,1)}), bf16[8,128,128]{1,2,0:T(8,128)(2,1)S(1)}, u32[]{:S(2)}, u32[]{:S(2)}) async-start(bf16[8,128,128]{1,2,0:T(8,128)(2,1)} %copy_bitcast_fusion), calls=%async_computation.1 | async-start | bytes 524288 | tf_op jit(solution)/shard_map/all_to_all | solution.py:54
  217.7 73.0 %all-to-all-start = ((bf16[4,128,128]{1,2,0:T(8,128)(2,1)}), bf16[4,128,128]{1,2,0:T(8,128)(2,1)S(1)}, u32[]{:S(2)}, u32[]{:S(2)}) async-start(bf16[4,128,128]{1,2,0:T(8,128)(2,1)} %copy_bitcast_fusion.1), calls=%async_computation | async-start | bytes 262144 | tf_op jit(solution)/shard_map/all_to_all | solution.py:51
Sparse Core Ops, SparseCore 0:
  9.9 55.3 all-gather.4
  66.9 82.0 all-gather.6
  150.6 87.1 all-gather.10
  239.5 51.1 all-gather.8

commit v2 on v1

--- a/solution.py
+++ b/solution.py
@@ -1,8 +1,11 @@
+import functools
 import math
 
 import jax
 import jax.numpy as jnp
 from jax import lax
+from jax.experimental import pallas as pl
+from jax.experimental.pallas import tpu as pltpu
 from jax.sharding import PartitionSpec as P
 
 
@@ -62,9 +65,554 @@
     return (query_grads, passage_grads, mean_loss)
 
 
+MESH = pl.DeviceIdType.MESH
+HALVES = 2
+CHUNKS = 8
+AHEAD = 3
+FIRST = 5
+
+
+def line_kernel(
+    blk_count,
+    q_ref,
+    p_ref,
+    ids_ref,
+    weight_ref,
+    qg_ref,
+    pg_ref,
+    loss_ref,
+    pp,
+    pq,
+    gp,
+    gq,
+    r_out,
+    r_in,
+    lp,
+    lt,
+    times,
+    pc,
+    tc,
+    ct,
+    tt,
+    cr,
+    ce,
+    tr,
+    loss_dp,
+    loss_blk,
+    s_pin,
+    s_pout,
+    s_psib,
+    r_p,
+    r_psib,
+    s_qin,
+    s_qsib,
+    r_q,
+    r_qsib,
+    s_r,
+    r_r,
+    s_gp,
+    r_gp,
+    s_gq,
+    r_gq,
+    s_c,
+    r_c,
+    r_e,
+    s_t,
+    r_t,
+    s_ld,
+    r_ld,
+    s_lb,
+    r_lb,
+):
+    b = lax.axis_index("blk")
+    d = lax.axis_index("dp")
+    rows, width = q_ref.shape
+    half = rows // HALVES
+    part = width // CHUNKS
+    hard_count = ids_ref.shape[1]
+    rescale = 4.0 / math.sqrt(width)
+    f32, bf16 = jnp.float32, jnp.bfloat16
+    z = lax.div(d, 2)
+    c = lax.rem(d, 2)
+    o = 1 - c
+    side = lax.div(z, 2)
+    se, sm = 3 * side, 1 + side
+    mp, ep = 3 - sm, 3 - se
+    sib = (b, 2 * z + o)
+    inner = (b, 2 * jnp.where(z == se, sm, mp) + c)
+    outer = (b, 2 * se + c)
+
+    barrier = pltpu.get_barrier_semaphore()
+    peers = [(b, lax.rem(d + i, 8)) for i in range(1, 8)]
+    others = [lax.rem(b + i, blk_count) for i in range(1, blk_count)]
+    peers += [(other, d) for other in others]
+    for peer in peers:
+        pl.semaphore_signal(barrier, inc=1, device_id=peer, device_id_type=MESH)
+
+    def core_rows(core):
+        return pl.ds(pl.multiple_of(core * rows, rows), rows)
+
+    pp[z, core_rows(c), :] = p_ref[...]
+    pq[z, core_rows(c), :] = q_ref[...]
+    gp[core_rows(b), :] = p_ref[...]
+    gq[core_rows(b), :] = q_ref[...]
+    pl.semaphore_wait(barrier, len(peers))
+
+    def remote(src, dst, send_sem, recv_sem, device):
+        return pltpu.make_async_remote_copy(
+            src_ref=src,
+            dst_ref=dst,
+            send_sem=send_sem,
+            recv_sem=recv_sem,
+            device_id=device,
+            device_id_type=MESH,
+        )
+
+    def p_slot(zz, core, h):
+        return pp.at[zz, pl.ds(pl.multiple_of(core * rows + h * half, half), half), :]
+
+    def q_slot(zz, core, j):
+        return pq.at[zz, core_rows(core), pl.ds(j * part, part)]
+
+    def p_src(zz, h, own):
+        return p_ref.at[pl.ds(h * half, half), :] if own else p_slot(zz, c, h)
+
+    def q_src(zz, j, own):
+        return q_ref.at[:, pl.ds(j * part, part)] if own else q_slot(zz, c, j)
+
+    def p_in(zz, h, own=False):
+        return remote(p_src(zz, h, own), p_slot(zz, c, h), s_pin.at[zz, h], r_p.at[zz, h], inner)
+
+    def p_out(zz, h, own=False):
+        return remote(p_src(zz, h, own), p_slot(zz, c, h), s_pout.at[zz, h], r_p.at[zz, h], outer)
+
+    def p_sib(zz, h, own=False):
+        return remote(p_src(zz, h, own), p_slot(zz, c, h), s_psib.at[zz, h], r_psib.at[zz, h], sib)
+
+    def q_in(zz, j, own=False):
+        return remote(q_src(zz, j, own), q_slot(zz, c, j), s_qin.at[zz, j], r_q.at[zz, j], inner)
+
+    def q_sib(zz, j, own=False):
+        return remote(q_src(zz, j, own), q_slot(zz, c, j), s_qsib.at[zz, j], r_qsib.at[zz, j], sib)
+
+    def wait_p(zz, h):
+        slot = p_slot(zz, c, h)
+        remote(slot, slot, s_pin.at[zz, h], r_p.at[zz, h], inner).wait_recv()
+
+    def wait_psib(zz):
+        for h in range(HALVES):
+            slot = p_slot(zz, o, h)
+            remote(slot, slot, s_psib.at[zz, h], r_psib.at[zz, h], sib).wait_recv()
+
+    def wait_q(zz, j):
+        slot = q_slot(zz, c, j)
+        remote(slot, slot, s_qin.at[zz, j], r_q.at[zz, j], inner).wait_recv()
+
+    def wait_qsib(zz, j):
+        slot = q_slot(zz, o, j)
+        remote(slot, slot, s_qsib.at[zz, j], r_qsib.at[zz, j], sib).wait_recv()
+
+    def r_copy(j):
+        cols = pl.ds(j * part, part)
+        return remote(r_out.at[:, cols], r_in.at[:, cols], s_r.at[j], r_r.at[j], outer)
+
+    def gp_copy(i):
+        return remote(p_ref, gp.at[core_rows(b), :], s_gp.at[i], r_gp.at[b], (others[i], d))
+
+    def gq_copy(i):
+        return remote(q_ref, gq.at[core_rows(b), :], s_gq.at[i], r_gq.at[b], (others[i], d))
+
+    def t_copy(i):
+        return remote(
+            tt.at[others[i]], tr.at[:, core_rows(b)], s_t.at[i], r_t.at[b], (others[i], d)
+        )
+
+    def ld_copy(i):
+        return remote(loss_dp.at[d], loss_dp.at[d], s_ld.at[i], r_ld.at[d], peers[i])
+
+    def lb_copy(i):
+        return remote(loss_blk.at[b], loss_blk.at[b], s_lb.at[i], r_lb.at[b], (others[i], d))
+
+    def wait_gp():
+        for i, other in enumerate(others):
+            slot = gp.at[core_rows(other), :]
+            remote(slot, slot, s_gp.at[i], r_gp.at[other], (other, d)).wait_recv()
+
+    def wait_gq_and_t():
+        for i, other in enumerate(others):
+            slot = gq.at[core_rows(other), :]
+            remote(slot, slot, s_gq.at[i], r_gq.at[other], (other, d)).wait_recv()
+            slot = tr.at[:, core_rows(other)]
+            remote(slot, slot, s_t.at[i], r_t.at[other], (other, d)).wait_recv()
+
+    def block_of(buf, sender):
+        zs, cs = lax.div(sender, 2), lax.rem(sender, 2)
+        return buf.at[zs, :, core_rows(cs)]
+
+    def wait_c(sender):
+        slot = block_of(cr, sender)
+        remote(slot, slot, s_c.at[0], r_c.at[sender], (b, sender)).wait_recv()
+
+    def wait_e(sender):
+        slot = block_of(ce, sender)
+        remote(slot, slot, s_c.at[0], r_e.at[sender], (b, sender)).wait_recv()
+
+    def c_copy(s, target):
+        return remote(ct.at[s], block_of(cr, d), s_c.at[s], r_c.at[d], (b, target))
+
+    def e_copy(s, target):
+        return remote(ct.at[s], block_of(ce, d), s_c.at[s], r_e.at[d], (b, target))
+
+    def each_coef(go):
+        for s in range(8):
+            zs, cs = s // 2, s % 2
+            if zs in (1, 2):
+                go(s, s, c_copy, cr, None)
+            else:
+                go(s, s, c_copy, cr, z == zs)
+                go(s, 2 * (1 if zs == 0 else 2) + cs, e_copy, ce, z != zs)
+
+    def start_coef(s, target, copy, buf, cond):
+        far = d != target
+        near = d == target
+        if cond is not None:
+            far, near = far & cond, near & cond
+
+        @pl.when(far)
+        def _():
+            copy(s, target).start()
+
+        @pl.when(near)
+        def _():
+            buf[z, :, core_rows(c)] = ct[s]
+
+    def end_coef(s, target, copy, buf, cond):
+        far = d != target
+        if cond is not None:
+            far = far & cond
+
+        @pl.when(far)
+        def _():
+            copy(s, target).wait_send()
+
+    nt = (((1,), (1,)), ((), ()))
+    step = min(512, width)
+
+    def pool_logits(zz):
+        def body(k, acc):
+            cols = pl.ds(pl.multiple_of(k * step, step), step)
+            return acc + lax.dot_general(
+                q_ref[:, cols], pp[zz, :, cols], nt, preferred_element_type=f32
+            )
+
+        zero = jnp.zeros((rows, 2 * rows), f32)
+        lp[zz] = lax.fori_loop(0, width // step, body, zero) * rescale
+
+    def tile_logits():
+        def body(k, acc):
+            cols = pl.ds(pl.multiple_of(k * step, step), step)
+            return acc + lax.dot_general(
+                q_ref[:, cols], gp[:, cols], nt, preferred_element_type=f32
+            )
+
+        zero = jnp.zeros((rows, blk_count * rows), f32)
+        lt[...] = lax.fori_loop(0, width // step, body, zero) * rescale
+
+    def count_ids():
+        for zz in range(4):
+            cols = lax.broadcasted_iota(jnp.int32, (rows, 2 * rows), 1) + zz * 2 * rows
+            total = jnp.zeros((rows, 2 * rows), f32)
+            for k in range(hard_count):
+                total += (ids_ref[:, k : k + 1] == cols).astype(f32)
+            times[zz] = total
+
+    def softmax():
+        tile = lt[...]
+        highest = jnp.max(tile, axis=1, keepdims=True)
+        for zz in range(4):
+            taken = jnp.where(times[zz] > 0.0, lp[zz], -jnp.inf)
+            highest = jnp.maximum(highest, jnp.max(taken, axis=1, keepdims=True))
+        sumexp = jnp.sum(jnp.exp(tile - highest), axis=1, keepdims=True)
+        for zz in range(4):
+            taken = jnp.where(times[zz] > 0.0, lp[zz], -jnp.inf)
+            sumexp += jnp.sum(times[zz] * jnp.exp(taken - highest), axis=1, keepdims=True)
+        lse = highest + jnp.log(sumexp)
+        weight = weight_ref[...]
+        coefs = rescale * weight
+        for zz in range(4):
+            taken = jnp.where(times[zz] > 0.0, lp[zz], -jnp.inf)
+            one = (coefs * jnp.exp(taken - lse)).astype(bf16).astype(f32)
+            many = times[zz] * one
+            pc[zz] = many.astype(bf16)
+            for core in range(2):
+                ct[2 * zz + core] = many[:, core * rows : (core + 1) * rows].T.astype(bf16)
+        each_coef(start_coef)
+        row = lax.broadcasted_iota(jnp.int32, tile.shape, 0) + b * rows
+        own = lax.broadcasted_iota(jnp.int32, tile.shape, 1) == row
+        coef = coefs * (jnp.exp(tile - lse) - own.astype(f32))
+        tc[...] = coef.astype(bf16)
+        for g in range(blk_count):
+            tt[g] = coef[:, g * rows : (g + 1) * rows].T.astype(bf16)
+        for i in range(len(others)):
+            t_copy(i).start()
+        tr[:, core_rows(b)] = tt[b]
+        positive = jnp.sum(jnp.where(own, tile, 0.0), axis=1, keepdims=True)
+        loss = jnp.sum(weight * (lse - positive), axis=0, keepdims=True)
+        loss_dp[d] = jnp.broadcast_to(loss, (8, 128))
+        for i in range(7):
+            ld_copy(i).start()
+
+    def query_grads():
+        @pl.loop(0, CHUNKS)
+        def _(j):
+            cols = pl.ds(pl.multiple_of(j * part, part), part)
+            acc = jnp.dot(tc[...], gp[:, cols], preferred_element_type=f32)
+            for zz in range(4):
+                acc += jnp.dot(pc[zz], pp[zz, :, cols], preferred_element_type=f32)
+            qg_ref[:, cols] = acc
+
+    def group():
+        wait_gp()
+        for i in range(len(others)):
+            gq_copy(i).start()
+        tile_logits()
+
+    for i in range(len(others)):
+        gp_copy(i).start()
+
+    @pl.when(z == sm)
+    def _():
+        for h in range(HALVES):
+            p_in(sm, h, True).start()
+            p_out(sm, h, True).start()
+            p_sib(sm, h, True).start()
+        count_ids()
+        wait_psib(sm)
+        pool_logits(sm)
+        for h in range(HALVES):
+            wait_p(se, h)
+            p_in(se, h).start()
+            p_sib(se, h).start()
+            wait_p(mp, h)
+            p_out(mp, h).start()
+            p_sib(mp, h).start()
+        for j in range(CHUNKS):
+            q_sib(sm, j, True).start()
+        wait_psib(se)
+        pool_logits(se)
+        wait_psib(mp)
+        pool_logits(mp)
+        for h in range(HALVES):
+            wait_p(ep, h)
+            p_out(ep, h).start()
+            p_sib(ep, h).start()
+        for j in range(AHEAD):
+            q_in(sm, j, True).start()
+        for j in range(CHUNKS):
+            wait_q(se, j)
+            if j < AHEAD:
+                q_in(se, j).start()
+            q_sib(se, j).start()
+        group()
+        wait_psib(ep)
+        pool_logits(ep)
+        softmax()
+        query_grads()
+
+        def end_grads(j):
+            wait_qsib(sm, j)
+            wait_qsib(mp, j)
+            wait_qsib(ep, j)
+            cols = pl.ds(j * part, part)
+            acc = jnp.zeros((rows, part), f32)
+            for t in range(1, 4):
+                zz = lax.rem(se + t, 4)
+                acc += jnp.dot(ce[zz], pq[zz, :, cols], preferred_element_type=f32)
+            r_out[:, cols] = acc.astype(bf16)
+            r_copy(j).start()
+
+        for j in range(CHUNKS):
+            wait_q(mp, j)
+            q_sib(mp, j).start()
+            wait_q(ep, j)
+            q_sib(ep, j).start()
+            if j + AHEAD < CHUNKS:
+                q_in(sm, j + AHEAD, True).start()
+                q_in(se, j + AHEAD).start()
+            if j == FIRST:
+                for t in range(1, 4):
+                    for core in range(2):
+                        sender = 2 * lax.rem(se + t, 4) + core
+
+                        @pl.when(sender != d)
+                        def _():
+                            wait_e(sender)
+
+                for i in range(FIRST):
+                    end_grads(i)
+            if j >= FIRST:
+                end_grads(j)
+        for j in range(CHUNKS):
+            wait_qsib(se, j)
+        for i in range(7):
+            wait_c(peers[i][1])
+        wait_gq_and_t()
+
+        @pl.loop(0, CHUNKS)
+        def _(j):
+            cols = pl.ds(pl.multiple_of(j * part, part), part)
+            acc = jnp.dot(tr[...], gq[:, cols], preferred_element_type=f32)
+            for zz in range(4):
+                acc += jnp.dot(cr[zz], pq[zz, :, cols], preferred_element_type=f32)
+            pg_ref[:, cols] = acc
+
+        for h in range(HALVES):
+            p_in(sm, h, True).wait_send()
+            p_out(sm, h, True).wait_send()
+            p_sib(sm, h, True).wait_send()
+            p_in(se, h).wait_send()
+            p_sib(se, h).wait_send()
+            p_out(mp, h).wait_send()
+            p_sib(mp, h).wait_send()
+            p_out(ep, h).wait_send()
+            p_sib(ep, h).wait_send()
+        for j in range(CHUNKS):
+            q_in(sm, j, True).wait_send()
+            q_in(se, j).wait_send()
+            q_sib(sm, j, True).wait_send()
+            q_sib(se, j).wait_send()
+            q_sib(mp, j).wait_send()
+            q_sib(ep, j).wait_send()
+            r_copy(j).wait_send()
+
+    @pl.when(z == se)
+    def _():
+        for h in range(HALVES):
+            p_in(se, h, True).start()
+            p_sib(se, h, True).start()
+        count_ids()
+        wait_psib(se)
+        pool_logits(se)
+        for h in range(HALVES):
+            p_in(se, h, True).wait_send()
+        for j in range(CHUNKS):
+            q_in(se, j, True).start()
+            q_sib(se, j, True).start()
+        for zz in (sm, mp, ep):
+            if zz is ep:
+                group()
+            for h in range(HALVES):
+                wait_p(zz, h)
+                p_sib(zz, h).start()
+            wait_psib(zz)
+            pool_logits(zz)
+        softmax()
+        query_grads()
+        for j in range(CHUNKS):
+            wait_qsib(se, j)
+        wait_c(2 * z + o)
+        wait_gq_and_t()
+
+        @pl.loop(0, CHUNKS)
+        def _(j):
+            cols = pl.ds(pl.multiple_of(j * part, part), part)
+            acc = jnp.dot(tr[...], gq[:, cols], preferred_element_type=f32)
+            pg_ref[:, cols] = acc + jnp.dot(cr[se], pq[se, :, cols], preferred_element_type=f32)
+
+        for j in range(CHUNKS):
+            cols = pl.ds(j * part, part)
+            r_slot = r_in.at[:, cols]
+            remote(r_slot, r_slot, s_r.at[j], r_r.at[j], inner).wait_recv()
+            pg_ref[:, cols] += r_in[:, cols].astype(f32)
+        for h in range(HALVES):
+            p_sib(se, h, True).wait_send()
+            for zz in (sm, mp, ep):
+                p_sib(zz, h).wait_send()
+        for j in range(CHUNKS):
+            q_in(se, j, True).wait_send()
+            q_sib(se, j, True).wait_send()
+
+    for i in range(7):
+        peer = peers[i][1]
+        slot = loss_dp.at[peer]
+        remote(slot, slot, s_ld.at[i], r_ld.at[peer], peers[i]).wait_recv()
+    total = loss_dp[0]
+    for s in range(1, 8):
+        total = total + loss_dp[s]
+    loss_blk[b] = total
+    for i in range(len(others)):
+        lb_copy(i).start()
+    for i, other in enumerate(others):
+        slot = loss_blk.at[other]
+        remote(slot, slot, s_lb.at[i], r_lb.at[other], (other, d)).wait_recv()
+    total = loss_blk[0]
+    for g in range(1, blk_count):
+        total = total + loss_blk[g]
+    loss_ref[...] = total / (rows * blk_count * 8)
+    each_coef(end_coef)
+    for i in range(len(others)):
+        gp_copy(i).wait_send()
+        gq_copy(i).wait_send()
+        t_copy(i).wait_send()
+        lb_copy(i).wait_send()
+    for i in range(7):
+        ld_copy(i).wait_send()
+
+
+def on_line(queries, passages, hard_ids, query_weight):
+    rows, width = queries.shape
+    blk_count = lax.axis_size("blk")
+    bf16, f32 = jnp.bfloat16, jnp.float32
+    dma = pltpu.SemaphoreType.DMA
+    vmem = pl.BlockSpec(memory_space=pltpu.VMEM)
+    query_grads, passage_grads, loss = pl.pallas_call(
+        functools.partial(line_kernel, blk_count),
+        out_shape=(
+            jax.ShapeDtypeStruct((rows, width), f32),
+            jax.ShapeDtypeStruct((rows, width), f32),
+            jax.ShapeDtypeStruct((8, 128), f32),
+        ),
+        in_specs=[vmem] * 4,
+        out_specs=(vmem, vmem, vmem),
+        scratch_shapes=[
+            pltpu.VMEM((4, 2 * rows, width), bf16),
+            pltpu.VMEM((4, 2 * rows, width), bf16),
+            pltpu.VMEM((blk_count * rows, width), bf16),
+            pltpu.VMEM((blk_count * rows, width), bf16),
+            pltpu.VMEM((rows, width), bf16),
+            pltpu.VMEM((rows, width), bf16),
+            pltpu.VMEM((4, rows, 2 * rows), f32),
+            pltpu.VMEM((rows, blk_count * rows), f32),
+            pltpu.VMEM((4, rows, 2 * rows), f32),
+            pltpu.VMEM((4, rows, 2 * rows), bf16),
+            pltpu.VMEM((rows, blk_count * rows), bf16),
+            pltpu.VMEM((8, rows, rows), bf16),
+            pltpu.VMEM((blk_count, rows, rows), bf16),
+            pltpu.VMEM((4, rows, 2 * rows), bf16),
+            pltpu.VMEM((4, rows, 2 * rows), bf16),
+            pltpu.VMEM((rows, blk_count * rows), bf16),
+            pltpu.VMEM((8, 8, 128), f32),
+            pltpu.VMEM((blk_count, 8, 128), f32),
+        ]
+        + [dma((4, HALVES))] * 5
+        + [dma((4, CHUNKS))] * 4
+        + [dma((CHUNKS,))] * 2
+        + [dma((blk_count,))] * 4
+        + [dma((8,))] * 3
+        + [dma((blk_count,))] * 2
+        + [dma((8,))] * 2
+        + [dma((blk_count,))] * 2,
+        compiler_params=pltpu.CompilerParams(
+            collective_id=0, has_side_effects=True, vmem_limit_bytes=56 * 1024 * 1024
+        ),
+    )(queries, passages, hard_ids, query_weight[:, None])
+    return (query_grads, passage_grads, loss[0, 0])
+
+
 def solution(mesh):
+    small = mesh.shape["dp"] == 8 and mesh.shape["blk"] <= 4
     return jax.shard_map(
-        pooled,
+        on_line if small else pooled,
         mesh=mesh,
         in_specs=(
             P(("blk", "dp"), None),

time: 303 us -> 136 us (0.45)
  waiting for transfers between devices: 202 us -> 0 us
  Pallas kernels: 0 us -> 127 us
  blocking collectives: 44.1 us -> 0 us
  matrix products: 29.2 us -> 0 us
  between operations: 15.6 us -> 0.64 us
  local copies, waits for them, and re-layouts: 0.02 us -> 8.57 us
  starting transfers between devices: 7.3 us -> 0 us
  other arithmetic: 3.96 us -> 0 us
    all_gather x4 -> x0, waiting for transfers between devices: 200 us -> none  [the longest x1 79.9 us: pooled(): pool_passages = lax.all_gather(passages, 'dp', axis=0, tiled=True)]
    pallas_call x0 -> x1, Pallas kernels: none -> 127 us  [on_line(): pl.pallas_call(functools.partial(line_kernel, blk_count), out_shape=(jax....]
    psum x1 -> x0, blocking collectives: 44.1 us -> none  [pooled(): lax.psum(loss_part, ('blk', 'dp')) / (rows_dev * blk_count * dp_count)]
    dot_general x6 -> x0, matrix products: 29.2 us -> none  [the longest x1 6.67 us: pooled(): lax.dot_general(queries, pool_passages, contract, preferred_element_type=...]
    all_to_all x2 -> x0, starting transfers between devices: 7.15 us -> none  [the longest x1 3.74 us: pooled(): lax.all_to_all(tile_coef.T.reshape(blk_count, rows_dev, rows_dev), 'blk',...]
    unnamed x8 -> x5, local copies, waits for them, and re-layouts: 0.02 us -> 6 us
  transfers between devices with their start and end apart: 6 -> 0, of which waited for: 4 -> 0; matrix products, arithmetic and copies ran while one was open for 10% -> 0% of each run, Pallas kernels for 0% -> 0%
where the time goes in v2:
time: 136 us
  Pallas kernels  127 us (93%)
  local copies, waits for them, and re-layouts  8.57 us (6%)
    pallas_call x1, Pallas kernels, on_line(): pl.pallas_call(functools.partial(line_kernel, blk_count), out_shape=(jax....  127 us
    unnamed x5, local copies, waits for them, and re-layouts  6 us

profile of v2, /device:TPU:0, one launch (start us, length us, event | category | flops | bytes accessed | tf_op | source)
XLA Modules:
  0.0 135.9 jit_solution(5444872069078810618)
XLA Ops:
  0.6 1.4 %copy.7.ids_ref = s32[128,8]{1,0:T(8,128)} copy(s32[128,8]{0,1:T(8,128)} %param.6) | data formatting | bytes 8192 | tf_op args[2]
  2.0 1.4 %copy.8.weight_ref = f32[128,1]{1,0:T(8,128)} copy(f32[128,1]{0,1:T(1,128)} %bitcast.2) | data formatting | bytes 1024 | tf_op jit(solution)/shard_map/broadcast_in_dim | solution.py:608
  3.4 126.7 %shard_map.67 = (f32[128,4096]{1,0:T(8,128)}, f32[128,4096]{1,0:T(8,128)}, f32[8,128]{1,0:T(8,128)}) custom-call(bf16[128,4096]{1,0:T(8,128)(2,1)} %q_ref.1, bf16[128,4096]{1,0:T(8,128)(2,1)} %p_ref.1, s32[128,8]{1,0:T(8,128)} %copy.7.ids_ref, f32[128,1]{1,0:T(8,128)} %copy.8.weight_ref), custom_call_target="tpu_custom_call" | custom-call | tf_op jit(solution)/shard_map/pallas_call | solution.py:568
  130.2 1.2 slice.3
  131.3 0.0 copy-start
  131.4 3.3 %copy.11 = f32[128,4096]{1,0:T(8,128)} copy(f32[128,4096]{1,0:T(8,128)} %get-tuple-element.12) | data formatting | bytes 4194304
  134.6 0.0 copy-done
  134.6 1.3 copy.12
Async XLA Ops:
  131.3 3.3 %copy-start = (f32[128,4096]{1,0:T(8,128)S(1)}, f32[128,4096]{1,0:T(8,128)}, u32[]{:S(2)}) copy-start(f32[128,4096]{1,0:T(8,128)} %get-tuple-element.13) | copy-start | bytes 6291460

commit v3 on v2

--- a/solution.py
+++ b/solution.py
@@ -68,8 +68,9 @@
 MESH = pl.DeviceIdType.MESH
 HALVES = 2
 CHUNKS = 8
-AHEAD = 3
-FIRST = 5
+AHEAD = 2
+FIRST = 3
+LAST = 5
 
 
 def line_kernel(
@@ -88,15 +89,18 @@
     r_out,
     r_in,
     lp,
+    le,
     lt,
-    times,
     pc,
     tc,
-    ct,
     tt,
-    cr,
+    cm,
     ce,
     tr,
+    meta,
+    hb,
+    st_out,
+    st_in,
     loss_dp,
     loss_blk,
     s_pin,
@@ -114,11 +118,14 @@
     r_gp,
     s_gq,
     r_gq,
-    s_c,
-    r_c,
-    r_e,
     s_t,
     r_t,
+    s_m,
+    r_m,
+    s_h,
+    r_h,
+    s_st,
+    r_st,
     s_ld,
     r_ld,
     s_lb,
@@ -129,7 +136,7 @@
     rows, width = q_ref.shape
     half = rows // HALVES
     part = width // CHUNKS
-    hard_count = ids_ref.shape[1]
+    hard_count = ids_ref.shape[0]
     rescale = 4.0 / math.sqrt(width)
     f32, bf16 = jnp.float32, jnp.bfloat16
     z = lax.div(d, 2)
@@ -156,6 +163,8 @@
     pq[z, core_rows(c), :] = q_ref[...]
     gp[core_rows(b), :] = p_ref[...]
     gq[core_rows(b), :] = q_ref[...]
+    meta[d, 0:hard_count, :] = ids_ref[...].astype(f32)
+    meta[d, hard_count:, :] = jnp.broadcast_to(weight_ref[...], (8, rows))
     pl.semaphore_wait(barrier, len(peers))
 
     def remote(src, dst, send_sem, recv_sem, device):
@@ -216,11 +225,49 @@
         cols = pl.ds(j * part, part)
         return remote(r_out.at[:, cols], r_in.at[:, cols], s_r.at[j], r_r.at[j], outer)
 
-    def gp_copy(i):
-        return remote(p_ref, gp.at[core_rows(b), :], s_gp.at[i], r_gp.at[b], (others[i], d))
-
-    def gq_copy(i):
-        return remote(q_ref, gq.at[core_rows(b), :], s_gq.at[i], r_gq.at[b], (others[i], d))
+    xn = b + 1 - 2 * lax.rem(b, 2)
+    yn = b + 2 - 4 * lax.div(b, 2)
+    near = (xn, yn)
+
+    def half_rows(owner, h):
+        return pl.ds(pl.multiple_of(owner * rows + h * half, half), half)
+
+    def g_copy(own, buf, s_sem, r_sem, n, h):
+        src = own.at[pl.ds(h * half, half), :]
+        dst = buf.at[half_rows(b, h), :]
+        return remote(src, dst, s_sem.at[n, h], r_sem.at[b, h], (near[n], d))
+
+    def g_relay(buf, s_sem, r_sem, n):
+        h = 1 - n
+        slot = buf.at[half_rows(near[1 - n], h), :]
+        return remote(slot, slot, s_sem.at[2, n], r_sem.at[near[1 - n], h], (near[n], d))
+
+    def g_wait(buf, s_sem, r_sem, owner, h):
+        slot = buf.at[half_rows(owner, h), :]
+        remote(slot, slot, s_sem.at[0, h], r_sem.at[owner, h], (xn, d)).wait_recv()
+
+    def g_start(own, buf, s_sem, r_sem):
+        for h in range(HALVES):
+            g_copy(own, buf, s_sem, r_sem, 0, h).start()
+            g_copy(own, buf, s_sem, r_sem, 1, 1 - h).start()
+
+    def g_forward(buf, s_sem, r_sem):
+        g_wait(buf, s_sem, r_sem, xn, 0)
+        g_relay(buf, s_sem, r_sem, 1).start()
+        g_wait(buf, s_sem, r_sem, yn, 1)
+        g_relay(buf, s_sem, r_sem, 0).start()
+
+    def g_finish(buf, s_sem, r_sem):
+        g_wait(buf, s_sem, r_sem, xn, 1)
+        g_wait(buf, s_sem, r_sem, yn, 0)
+        g_wait(buf, s_sem, r_sem, 3 - b, 0)
+        g_wait(buf, s_sem, r_sem, 3 - b, 1)
+
+    def g_sent(own, buf, s_sem, r_sem):
+        for n in range(2):
+            for h in range(HALVES):
+                g_copy(own, buf, s_sem, r_sem, n, h).wait_send()
+            g_relay(buf, s_sem, r_sem, n).wait_send()
 
     def t_copy(i):
         return remote(
@@ -233,67 +280,31 @@
     def lb_copy(i):
         return remote(loss_blk.at[b], loss_blk.at[b], s_lb.at[i], r_lb.at[b], (others[i], d))
 
-    def wait_gp():
+    def wait_t():
         for i, other in enumerate(others):
-            slot = gp.at[core_rows(other), :]
-            remote(slot, slot, s_gp.at[i], r_gp.at[other], (other, d)).wait_recv()
-
-    def wait_gq_and_t():
-        for i, other in enumerate(others):
-            slot = gq.at[core_rows(other), :]
-            remote(slot, slot, s_gq.at[i], r_gq.at[other], (other, d)).wait_recv()
             slot = tr.at[:, core_rows(other)]
             remote(slot, slot, s_t.at[i], r_t.at[other], (other, d)).wait_recv()
 
-    def block_of(buf, sender):
-        zs, cs = lax.div(sender, 2), lax.rem(sender, 2)
-        return buf.at[zs, :, core_rows(cs)]
-
-    def wait_c(sender):
-        slot = block_of(cr, sender)
-        remote(slot, slot, s_c.at[0], r_c.at[sender], (b, sender)).wait_recv()
-
-    def wait_e(sender):
-        slot = block_of(ce, sender)
-        remote(slot, slot, s_c.at[0], r_e.at[sender], (b, sender)).wait_recv()
-
-    def c_copy(s, target):
-        return remote(ct.at[s], block_of(cr, d), s_c.at[s], r_c.at[d], (b, target))
-
-    def e_copy(s, target):
-        return remote(ct.at[s], block_of(ce, d), s_c.at[s], r_e.at[d], (b, target))
-
-    def each_coef(go):
-        for s in range(8):
-            zs, cs = s // 2, s % 2
-            if zs in (1, 2):
-                go(s, s, c_copy, cr, None)
-            else:
-                go(s, s, c_copy, cr, z == zs)
-                go(s, 2 * (1 if zs == 0 else 2) + cs, e_copy, ce, z != zs)
-
-    def start_coef(s, target, copy, buf, cond):
-        far = d != target
-        near = d == target
-        if cond is not None:
-            far, near = far & cond, near & cond
-
-        @pl.when(far)
-        def _():
-            copy(s, target).start()
-
-        @pl.when(near)
-        def _():
-            buf[z, :, core_rows(c)] = ct[s]
-
-    def end_coef(s, target, copy, buf, cond):
-        far = d != target
-        if cond is not None:
-            far = far & cond
-
-        @pl.when(far)
-        def _():
-            copy(s, target).wait_send()
+    def m_copy(host):
+        return remote(meta.at[d], meta.at[d], s_m.at[host - 2], r_m.at[d], (b, host))
+
+    def wait_m(sender):
+        slot = meta.at[sender]
+        remote(slot, slot, s_m.at[0], r_m.at[sender], (b, sender)).wait_recv()
+
+    hosts = (2 * sm + o, 2 * mp + c, 2 * mp + o)
+    end_dev = 2 * se + c
+
+    def h_copy(n, owner, mine):
+        slot = hb.at[owner]
+        return remote(slot, slot, s_h.at[mine, n], r_h.at[owner], (b, hosts[n]))
+
+    def wait_h(owner):
+        slot = hb.at[owner]
+        remote(slot, slot, s_h.at[0, 0], r_h.at[owner], sib).wait_recv()
+
+    def st_copy():
+        return remote(st_out, st_in, s_st.at[0], r_st.at[0], inner)
 
     nt = (((1,), (1,)), ((), ()))
     step = min(512, width)
@@ -308,6 +319,18 @@
         zero = jnp.zeros((rows, 2 * rows), f32)
         lp[zz] = lax.fori_loop(0, width // step, body, zero) * rescale
 
+    def end_logits():
+        @pl.loop(0, 4)
+        def _(zz):
+            def body(k, acc):
+                cols = pl.ds(pl.multiple_of(k * step, step), step)
+                return acc + lax.dot_general(
+                    pq[se, core_rows(c), cols], pp[zz, :, cols], nt, preferred_element_type=f32
+                )
+
+            zero = jnp.zeros((rows, 2 * rows), f32)
+            le[zz] = lax.fori_loop(0, width // step, body, zero) * rescale
+
     def tile_logits():
         def body(k, acc):
             cols = pl.ds(pl.multiple_of(k * step, step), step)
@@ -318,38 +341,44 @@
         zero = jnp.zeros((rows, blk_count * rows), f32)
         lt[...] = lax.fori_loop(0, width // step, body, zero) * rescale
 
-    def count_ids():
-        for zz in range(4):
-            cols = lax.broadcasted_iota(jnp.int32, (rows, 2 * rows), 1) + zz * 2 * rows
+    def columns_of(device):
+        rest = jnp.zeros((rows - hard_count - 8, rows), f32)
+        return jnp.concatenate([meta[device], rest], axis=0).T
+
+    lanes = lax.broadcasted_iota(jnp.int32, (rows, rows), 1)
+
+    def pool_ids(zz):
+        iota = lax.broadcasted_iota(jnp.int32, (rows, 2 * rows), 1)
+        return (iota + zz * 2 * rows).astype(f32)
+
+    def hard_logits(logits, info):
+        found = jnp.full((rows, rows), -jnp.inf, f32)
+        for k in range(hard_count):
             total = jnp.zeros((rows, 2 * rows), f32)
-            for k in range(hard_count):
-                total += (ids_ref[:, k : k + 1] == cols).astype(f32)
-            times[zz] = total
-
-    def softmax():
+            for zz in range(4):
+                total += jnp.where(pool_ids(zz) == info[:, k : k + 1], logits[zz], 0.0)
+            found = jnp.where(lanes == k, jnp.sum(total, axis=1, keepdims=True), found)
+        return found
+
+    def row_stats():
+        top = jnp.max(lt[...], axis=1, keepdims=True)
+        return top, jnp.sum(jnp.exp(lt[...] - top), axis=1, keepdims=True)
+
+    def hard_softmax(logits, info, top, total):
+        found = hard_logits(logits, info)
+        highest = jnp.maximum(top, jnp.max(found, axis=1, keepdims=True))
+        sumexp = total * jnp.exp(top - highest)
+        sumexp += jnp.sum(jnp.exp(found - highest), axis=1, keepdims=True)
+        lse = highest + jnp.log(sumexp)
+        coefs = rescale * info[:, hard_count : hard_count + 1]
+        return lse, (coefs * jnp.exp(found - lse)).astype(bf16).astype(f32)
+
+    def query_side(info, lse, hard):
+        weight = info[:, hard_count : hard_count + 1]
         tile = lt[...]
-        highest = jnp.max(tile, axis=1, keepdims=True)
-        for zz in range(4):
-            taken = jnp.where(times[zz] > 0.0, lp[zz], -jnp.inf)
-            highest = jnp.maximum(highest, jnp.max(taken, axis=1, keepdims=True))
-        sumexp = jnp.sum(jnp.exp(tile - highest), axis=1, keepdims=True)
-        for zz in range(4):
-            taken = jnp.where(times[zz] > 0.0, lp[zz], -jnp.inf)
-            sumexp += jnp.sum(times[zz] * jnp.exp(taken - highest), axis=1, keepdims=True)
-        lse = highest + jnp.log(sumexp)
-        weight = weight_ref[...]
-        coefs = rescale * weight
-        for zz in range(4):
-            taken = jnp.where(times[zz] > 0.0, lp[zz], -jnp.inf)
-            one = (coefs * jnp.exp(taken - lse)).astype(bf16).astype(f32)
-            many = times[zz] * one
-            pc[zz] = many.astype(bf16)
-            for core in range(2):
-                ct[2 * zz + core] = many[:, core * rows : (core + 1) * rows].T.astype(bf16)
-        each_coef(start_coef)
         row = lax.broadcasted_iota(jnp.int32, tile.shape, 0) + b * rows
         own = lax.broadcasted_iota(jnp.int32, tile.shape, 1) == row
-        coef = coefs * (jnp.exp(tile - lse) - own.astype(f32))
+        coef = rescale * weight * (jnp.exp(tile - lse) - own.astype(f32))
         tc[...] = coef.astype(bf16)
         for g in range(blk_count):
             tt[g] = coef[:, g * rows : (g + 1) * rows].T.astype(bf16)
@@ -361,6 +390,25 @@
         loss_dp[d] = jnp.broadcast_to(loss, (8, 128))
         for i in range(7):
             ld_copy(i).start()
+        for zz in range(4):
+            total = jnp.zeros((rows, 2 * rows), f32)
+            for k in range(hard_count):
+                total += jnp.where(pool_ids(zz) == info[:, k : k + 1], hard[:, k : k + 1], 0.0)
+            pc[zz] = total.astype(bf16)
+
+    def passage_side(buf, owner):
+        iota = lax.broadcasted_iota(jnp.int32, (rows, rows), 0)
+        ids = (iota + owner * rows).astype(f32)
+
+        @pl.loop(0, 4)
+        def _(zz):
+            for core in range(2):
+                dev = 2 * zz + core
+                total = jnp.zeros((rows, rows), f32)
+                for k in range(hard_count):
+                    hit = meta[dev, k : k + 1, :] == ids
+                    total += jnp.where(hit, hb[dev, k : k + 1, :], 0.0)
+                buf[zz, :, core * rows : (core + 1) * rows] = total.astype(bf16)
 
     def query_grads():
         @pl.loop(0, CHUNKS)
@@ -372,23 +420,36 @@
             qg_ref[:, cols] = acc
 
     def group():
-        wait_gp()
-        for i in range(len(others)):
-            gq_copy(i).start()
+        g_finish(gp, s_gp, r_gp)
+        g_start(q_ref, gq, s_gq, r_gq)
         tile_logits()
 
-    for i in range(len(others)):
-        gp_copy(i).start()
+    def tile_grads():
+        g_finish(gq, s_gq, r_gq)
+        wait_t()
+
+        @pl.loop(0, CHUNKS)
+        def _(j):
+            cols = pl.ds(pl.multiple_of(j * part, part), part)
+            pg_ref[:, cols] = jnp.dot(tr[...], gq[:, cols], preferred_element_type=f32)
 
     @pl.when(z == sm)
     def _():
         for h in range(HALVES):
             p_in(sm, h, True).start()
+        g_start(p_ref, gp, s_gp, r_gp)
+        for h in range(HALVES):
             p_out(sm, h, True).start()
             p_sib(sm, h, True).start()
-        count_ids()
+        for host in range(2, 6):
+
+            @pl.when(host != d)
+            def _():
+                m_copy(host).start()
+
         wait_psib(sm)
         pool_logits(sm)
+        g_forward(gp, s_gp, r_gp)
         for h in range(HALVES):
             wait_p(se, h)
             p_in(se, h).start()
@@ -398,10 +459,14 @@
             p_sib(mp, h).start()
         for j in range(CHUNKS):
             q_sib(sm, j, True).start()
+        for i in range(7):
+            wait_m(peers[i][1])
         wait_psib(se)
         pool_logits(se)
         wait_psib(mp)
         pool_logits(mp)
+        group()
+        top, total = row_stats()
         for h in range(HALVES):
             wait_p(ep, h)
             p_out(ep, h).start()
@@ -413,25 +478,21 @@
             if j < AHEAD:
                 q_in(se, j).start()
             q_sib(se, j).start()
-        group()
         wait_psib(ep)
         pool_logits(ep)
-        softmax()
-        query_grads()
-
-        def end_grads(j):
-            wait_qsib(sm, j)
-            wait_qsib(mp, j)
-            wait_qsib(ep, j)
-            cols = pl.ds(j * part, part)
-            acc = jnp.zeros((rows, part), f32)
-            for t in range(1, 4):
-                zz = lax.rem(se + t, 4)
-                acc += jnp.dot(ce[zz], pq[zz, :, cols], preferred_element_type=f32)
-            r_out[:, cols] = acc.astype(bf16)
-            r_copy(j).start()
-
-        for j in range(CHUNKS):
+        info = columns_of(d)
+        lse, hard = hard_softmax(lp, info, top, total)
+        hb[d] = hard.T[0:hard_count, :]
+        for n in range(3):
+            h_copy(n, d, 0).start()
+        end_logits()
+        remote(st_in, st_in, s_st.at[0], r_st.at[0], outer).wait_recv()
+        end_hard = hard_softmax(le, columns_of(end_dev), st_in[:, 0:1], st_in[:, 1:2])[1]
+        hb[end_dev] = end_hard.T[0:hard_count, :]
+        for n in range(3):
+            h_copy(n, end_dev, 1).start()
+
+        def q_step(j):
             wait_q(mp, j)
             q_sib(mp, j).start()
             wait_q(ep, j)
@@ -439,32 +500,45 @@
             if j + AHEAD < CHUNKS:
                 q_in(sm, j + AHEAD, True).start()
                 q_in(se, j + AHEAD).start()
+
+        def end_grads(j):
+            for zz in (se, sm, mp, ep):
+                wait_qsib(zz, j)
+            cols = pl.ds(j * part, part)
+            acc = jnp.zeros((rows, part), f32)
+            for zz in range(4):
+                acc += jnp.dot(ce[zz], pq[zz, :, cols], preferred_element_type=f32)
+            r_out[:, cols] = acc.astype(bf16)
+            r_copy(j).start()
+
+        def own_grads(j):
+            cols = pl.ds(j * part, part)
+            acc = pg_ref[:, cols]
+            for zz in range(4):
+                acc += jnp.dot(cm[zz], pq[zz, :, cols], preferred_element_type=f32)
+            pg_ref[:, cols] = acc
+
+        q_step(0)
+        query_side(info, lse, hard)
+        g_forward(gq, s_gq, r_gq)
+        query_grads()
+        for j in range(1, CHUNKS):
+            q_step(j)
             if j == FIRST:
-                for t in range(1, 4):
-                    for core in range(2):
-                        sender = 2 * lax.rem(se + t, 4) + core
-
-                        @pl.when(sender != d)
-                        def _():
-                            wait_e(sender)
-
+                for dev in (2 * sm + o, 2 * se + o, 2 * mp, 2 * mp + 1, 2 * ep, 2 * ep + 1):
+                    wait_h(dev)
+                passage_side(ce, end_dev)
                 for i in range(FIRST):
                     end_grads(i)
+                passage_side(cm, d)
             if j >= FIRST:
                 end_grads(j)
-        for j in range(CHUNKS):
-            wait_qsib(se, j)
-        for i in range(7):
-            wait_c(peers[i][1])
-        wait_gq_and_t()
-
-        @pl.loop(0, CHUNKS)
-        def _(j):
-            cols = pl.ds(pl.multiple_of(j * part, part), part)
-            acc = jnp.dot(tr[...], gq[:, cols], preferred_element_type=f32)
-            for zz in range(4):
-                acc += jnp.dot(cr[zz], pq[zz, :, cols], preferred_element_type=f32)
-            pg_ref[:, cols] = acc
+            if j == LAST:
+                tile_grads()
+                for i in range(LAST):
+                    own_grads(i)
+            if j >= LAST:
+                own_grads(j)
 
         for h in range(HALVES):
             p_in(sm, h, True).wait_send()
@@ -484,53 +558,65 @@
             q_sib(mp, j).wait_send()
             q_sib(ep, j).wait_send()
             r_copy(j).wait_send()
+        for n in range(3):
+            h_copy(n, d, 0).wait_send()
+            h_copy(n, end_dev, 1).wait_send()
 
     @pl.when(z == se)
     def _():
         for h in range(HALVES):
             p_in(se, h, True).start()
+        g_start(p_ref, gp, s_gp, r_gp)
+        for h in range(HALVES):
             p_sib(se, h, True).start()
-        count_ids()
+        for host in range(2, 6):
+            m_copy(host).start()
         wait_psib(se)
         pool_logits(se)
+        g_forward(gp, s_gp, r_gp)
         for h in range(HALVES):
             p_in(se, h, True).wait_send()
         for j in range(CHUNKS):
             q_in(se, j, True).start()
-            q_sib(se, j, True).start()
-        for zz in (sm, mp, ep):
-            if zz is ep:
-                group()
-            for h in range(HALVES):
-                wait_p(zz, h)
-                p_sib(zz, h).start()
-            wait_psib(zz)
-            pool_logits(zz)
-        softmax()
+
+        def receive(zz, h):
+            wait_p(zz, h)
+            p_sib(zz, h).start()
+
+        receive(sm, 0)
+        receive(sm, 1)
+        wait_psib(sm)
+        pool_logits(sm)
+        group()
+        top, total = row_stats()
+        st_out[...] = jnp.where(lanes == 0, top, total)
+        st_copy().start()
+        receive(mp, 0)
+        receive(mp, 1)
+        wait_psib(mp)
+        pool_logits(mp)
+        receive(ep, 0)
+        g_forward(gq, s_gq, r_gq)
+        receive(ep, 1)
+        wait_psib(ep)
+        pool_logits(ep)
+        info = columns_of(d)
+        lse, hard = hard_softmax(lp, info, top, total)
+        query_side(info, lse, hard)
         query_grads()
-        for j in range(CHUNKS):
-            wait_qsib(se, j)
-        wait_c(2 * z + o)
-        wait_gq_and_t()
-
-        @pl.loop(0, CHUNKS)
-        def _(j):
-            cols = pl.ds(pl.multiple_of(j * part, part), part)
-            acc = jnp.dot(tr[...], gq[:, cols], preferred_element_type=f32)
-            pg_ref[:, cols] = acc + jnp.dot(cr[se], pq[se, :, cols], preferred_element_type=f32)
-
+        tile_grads()
         for j in range(CHUNKS):
             cols = pl.ds(j * part, part)
             r_slot = r_in.at[:, cols]
             remote(r_slot, r_slot, s_r.at[j], r_r.at[j], inner).wait_recv()
             pg_ref[:, cols] += r_in[:, cols].astype(f32)
+        st_copy().wait_send()
         for h in range(HALVES):
             p_sib(se, h, True).wait_send()
             for zz in (sm, mp, ep):
                 p_sib(zz, h).wait_send()
         for j in range(CHUNKS):
             q_in(se, j, True).wait_send()
-            q_sib(se, j, True).wait_send()
 
     for i in range(7):
         peer = peers[i][1]
@@ -548,20 +634,25 @@
     total = loss_blk[0]
     for g in range(1, blk_count):
         total = total + loss_blk[g]
-    loss_ref[...] = total / (rows * blk_count * 8)
-    each_coef(end_coef)
+    loss_ref[0, 0] = jnp.max(total) / (rows * blk_count * 8)
     for i in range(len(others)):
-        gp_copy(i).wait_send()
-        gq_copy(i).wait_send()
         t_copy(i).wait_send()
         lb_copy(i).wait_send()
     for i in range(7):
         ld_copy(i).wait_send()
+    g_sent(p_ref, gp, s_gp, r_gp)
+    g_sent(q_ref, gq, s_gq, r_gq)
+    for host in range(2, 6):
+
+        @pl.when(host != d)
+        def _():
+            m_copy(host).wait_send()
 
 
 def on_line(queries, passages, hard_ids, query_weight):
     rows, width = queries.shape
     blk_count = lax.axis_size("blk")
+    hard_count = hard_ids.shape[1]
     bf16, f32 = jnp.bfloat16, jnp.float32
     dma = pltpu.SemaphoreType.DMA
     vmem = pl.BlockSpec(memory_space=pltpu.VMEM)
@@ -570,10 +661,10 @@
         out_shape=(
             jax.ShapeDtypeStruct((rows, width), f32),
             jax.ShapeDtypeStruct((rows, width), f32),
-            jax.ShapeDtypeStruct((8, 128), f32),
+            jax.ShapeDtypeStruct((1, 1), f32),
         ),
         in_specs=[vmem] * 4,
-        out_specs=(vmem, vmem, vmem),
+        out_specs=(vmem, vmem, pl.BlockSpec(memory_space=pltpu.SMEM)),
         scratch_shapes=[
             pltpu.VMEM((4, 2 * rows, width), bf16),
             pltpu.VMEM((4, 2 * rows, width), bf16),
@@ -582,35 +673,40 @@
             pltpu.VMEM((rows, width), bf16),
             pltpu.VMEM((rows, width), bf16),
             pltpu.VMEM((4, rows, 2 * rows), f32),
+            pltpu.VMEM((4, rows, 2 * rows), f32),
             pltpu.VMEM((rows, blk_count * rows), f32),
-            pltpu.VMEM((4, rows, 2 * rows), f32),
             pltpu.VMEM((4, rows, 2 * rows), bf16),
             pltpu.VMEM((rows, blk_count * rows), bf16),
-            pltpu.VMEM((8, rows, rows), bf16),
             pltpu.VMEM((blk_count, rows, rows), bf16),
             pltpu.VMEM((4, rows, 2 * rows), bf16),
             pltpu.VMEM((4, rows, 2 * rows), bf16),
             pltpu.VMEM((rows, blk_count * rows), bf16),
+            pltpu.VMEM((8, hard_count + 8, rows), f32),
+            pltpu.VMEM((8, hard_count, rows), f32),
+            pltpu.VMEM((rows, rows), f32),
+            pltpu.VMEM((rows, rows), f32),
             pltpu.VMEM((8, 8, 128), f32),
             pltpu.VMEM((blk_count, 8, 128), f32),
         ]
         + [dma((4, HALVES))] * 5
         + [dma((4, CHUNKS))] * 4
         + [dma((CHUNKS,))] * 2
-        + [dma((blk_count,))] * 4
-        + [dma((8,))] * 3
+        + [dma((3, HALVES)), dma((blk_count, HALVES))] * 2
         + [dma((blk_count,))] * 2
+        + [dma((4,)), dma((8,))]
+        + [dma((2, 3)), dma((8,))]
+        + [dma((1,))] * 2
         + [dma((8,))] * 2
         + [dma((blk_count,))] * 2,
         compiler_params=pltpu.CompilerParams(
-            collective_id=0, has_side_effects=True, vmem_limit_bytes=56 * 1024 * 1024
+            collective_id=0, has_side_effects=True, vmem_limit_bytes=44 * 1024 * 1024
         ),
-    )(queries, passages, hard_ids, query_weight[:, None])
-    return (query_grads, passage_grads, loss[0, 0])
+    )(queries, passages, hard_ids.T, query_weight[None, :])
+    return (query_grads, passage_grads, loss.reshape(()))
 
 
 def solution(mesh):
-    small = mesh.shape["dp"] == 8 and mesh.shape["blk"] <= 4
+    small = mesh.shape["dp"] == 8 and mesh.shape["blk"] == 4
     return jax.shard_map(
         on_line if small else pooled,
         mesh=mesh,

time: 136 us -> 125 us (0.919)
  Pallas kernels: 127 us -> 116 us
  local copies, waits for them, and re-layouts: 8.57 us -> 6.42 us
  between operations: 0.64 us -> 2.4 us
    pallas_call x1, Pallas kernels: 127 us -> 116 us  [on_line(): pl.pallas_call(functools.partial(line_kernel, blk_count), out_shape=(jax....]
    broadcast_in_dim x1 -> x0, local copies, waits for them, and re-layouts: 1.39 us -> none  [on_line(): query_weight[:, None]]
    unnamed x5 -> x10, local copies, waits for them, and re-layouts: 6 us -> 6.42 us
where the time goes in v3:
time: 125 us
  Pallas kernels  116 us (93%)
  local copies, waits for them, and re-layouts  6.42 us (5%)
  between operations  2.4 us (2%)
    pallas_call x1, Pallas kernels, on_line(): pl.pallas_call(functools.partial(line_kernel, blk_count), out_shape=(jax....  116 us
    unnamed x10, local copies, waits for them, and re-layouts  6.42 us

profile of v3, /device:TPU:0, one launch (start us, length us, event | category | flops | bytes accessed | tf_op | source)
XLA Modules:
  0.0 125.0 jit_solution(8195978249324554350)
XLA Ops:
  0.6 0.0 copy-start
  0.6 1.2 copy-done
  1.9 0.0 copy-start.1
  1.9 1.2 copy-done.1
  3.1 0.0 copy-start.2
  3.1 0.7 copy-done.2
  3.8 0.0 copy-start.3
  3.8 0.7 copy-done.3
  4.4 116.2 %shard_map.67 = (f32[128,4096]{1,0:T(8,128)S(1)}, f32[128,4096]{1,0:T(8,128)S(1)}, f32[1,1]{1,0:T(1,128)}) custom-call(bf16[128,4096]{1,0:T(8,128)(2,1)S(1)} %copy-done, bf16[128,4096]{1,0:T(8,128)(2,1)S(1)} %copy-done.1, s32[8,128]{1,0:T(8,128)S(1)} %bitcast.3, f32[1,128]{1,0:T(1,128)S(1)} %bitcast.4), custom_call_target="tpu_custom_call" | custom-call | tf_op jit(solution)/shard_map/pallas_call | solution.py:659
  120.6 1.3 %copy.10 = f32[128,4096]{1,0:T(8,128)} copy(f32[128,4096]{1,0:T(8,128)S(1)} %get-tuple-element.12) | data formatting | bytes 4194304
  121.9 1.3 %copy.11 = f32[128,4096]{1,0:T(8,128)} copy(f32[128,4096]{1,0:T(8,128)S(1)} %get-tuple-element.13) | data formatting | bytes 4194304
Async XLA Ops:
  0.6 1.2 copy-start
  1.9 1.2 copy-start.1
  3.1 0.7 copy-start.2
  3.8 0.7 copy-start.3

commit v4 on v3

--- a/solution.py
+++ b/solution.py
@@ -68,7 +68,7 @@
 MESH = pl.DeviceIdType.MESH
 HALVES = 2
 CHUNKS = 8
-AHEAD = 2
+AHEAD = 3
 FIRST = 3
 LAST = 5
 
@@ -130,6 +130,9 @@
     r_ld,
     s_lb,
     r_lb,
+    ids_v,
+    weight_v,
+    s_own,
 ):
     b = lax.axis_index("blk")
     d = lax.axis_index("dp")
@@ -159,13 +162,28 @@
     def core_rows(core):
         return pl.ds(pl.multiple_of(core * rows, rows), rows)
 
-    pp[z, core_rows(c), :] = p_ref[...]
-    pq[z, core_rows(c), :] = q_ref[...]
-    gp[core_rows(b), :] = p_ref[...]
-    gq[core_rows(b), :] = q_ref[...]
-    meta[d, 0:hard_count, :] = ids_ref[...].astype(f32)
-    meta[d, hard_count:, :] = jnp.broadcast_to(weight_ref[...], (8, rows))
+    local = [
+        pltpu.make_async_copy(src, dst, s_own.at[i])
+        for i, (src, dst) in enumerate(
+            (
+                (ids_ref, ids_v),
+                (weight_ref, weight_v),
+                (p_ref, pp.at[z, core_rows(c), :]),
+                (q_ref, gq.at[core_rows(b), :]),
+                (p_ref, gp.at[core_rows(b), :]),
+                (q_ref, pq.at[z, core_rows(c), :]),
+            )
+        )
+    ]
+    for copy in local:
+        copy.start()
     pl.semaphore_wait(barrier, len(peers))
+
+    def take_own():
+        for copy in local:
+            copy.wait()
+        meta[d, 0:hard_count, :] = ids_v[...].astype(f32)
+        meta[d, hard_count:, :] = jnp.broadcast_to(weight_v[...], (8, rows))
 
     def remote(src, dst, send_sem, recv_sem, device):
         return pltpu.make_async_remote_copy(
@@ -313,7 +331,7 @@
         def body(k, acc):
             cols = pl.ds(pl.multiple_of(k * step, step), step)
             return acc + lax.dot_general(
-                q_ref[:, cols], pp[zz, :, cols], nt, preferred_element_type=f32
+                gq[core_rows(b), cols], pp[zz, :, cols], nt, preferred_element_type=f32
             )
 
         zero = jnp.zeros((rows, 2 * rows), f32)
@@ -335,7 +353,7 @@
         def body(k, acc):
             cols = pl.ds(pl.multiple_of(k * step, step), step)
             return acc + lax.dot_general(
-                q_ref[:, cols], gp[:, cols], nt, preferred_element_type=f32
+                gq[core_rows(b), cols], gp[:, cols], nt, preferred_element_type=f32
             )
 
         zero = jnp.zeros((rows, blk_count * rows), f32)
@@ -441,6 +459,7 @@
         for h in range(HALVES):
             p_out(sm, h, True).start()
             p_sib(sm, h, True).start()
+        take_own()
         for host in range(2, 6):
 
             @pl.when(host != d)
@@ -471,13 +490,24 @@
             wait_p(ep, h)
             p_out(ep, h).start()
             p_sib(ep, h).start()
-        for j in range(AHEAD):
-            q_in(sm, j, True).start()
+            if h == 0:
+                q_in(sm, 0, True).start()
         for j in range(CHUNKS):
+            if 0 < j < AHEAD:
+                q_in(sm, j, True).start()
             wait_q(se, j)
             if j < AHEAD:
                 q_in(se, j).start()
             q_sib(se, j).start()
+        def q_step(j):
+            wait_q(mp, j)
+            q_sib(mp, j).start()
+            wait_q(ep, j)
+            q_sib(ep, j).start()
+            if j + AHEAD < CHUNKS:
+                q_in(sm, j + AHEAD, True).start()
+                q_in(se, j + AHEAD).start()
+
         wait_psib(ep)
         pool_logits(ep)
         info = columns_of(d)
@@ -486,20 +516,12 @@
         for n in range(3):
             h_copy(n, d, 0).start()
         end_logits()
+        q_step(0)
         remote(st_in, st_in, s_st.at[0], r_st.at[0], outer).wait_recv()
         end_hard = hard_softmax(le, columns_of(end_dev), st_in[:, 0:1], st_in[:, 1:2])[1]
         hb[end_dev] = end_hard.T[0:hard_count, :]
         for n in range(3):
             h_copy(n, end_dev, 1).start()
-
-        def q_step(j):
-            wait_q(mp, j)
-            q_sib(mp, j).start()
-            wait_q(ep, j)
-            q_sib(ep, j).start()
-            if j + AHEAD < CHUNKS:
-                q_in(sm, j + AHEAD, True).start()
-                q_in(se, j + AHEAD).start()
 
         def end_grads(j):
             for zz in (se, sm, mp, ep):
@@ -518,11 +540,12 @@
                 acc += jnp.dot(cm[zz], pq[zz, :, cols], preferred_element_type=f32)
             pg_ref[:, cols] = acc
 
-        q_step(0)
+        q_step(1)
         query_side(info, lse, hard)
         g_forward(gq, s_gq, r_gq)
+        q_step(2)
         query_grads()
-        for j in range(1, CHUNKS):
+        for j in range(3, CHUNKS):
             q_step(j)
             if j == FIRST:
                 for dev in (2 * sm + o, 2 * se + o, 2 * mp, 2 * mp + 1, 2 * ep, 2 * ep + 1):
@@ -569,6 +592,7 @@
         g_start(p_ref, gp, s_gp, r_gp)
         for h in range(HALVES):
             p_sib(se, h, True).start()
+        take_own()
         for host in range(2, 6):
             m_copy(host).start()
         wait_psib(se)
@@ -663,7 +687,7 @@
             jax.ShapeDtypeStruct((rows, width), f32),
             jax.ShapeDtypeStruct((1, 1), f32),
         ),
-        in_specs=[vmem] * 4,
+        in_specs=[pl.BlockSpec(memory_space=pltpu.HBM)] * 4,
         out_specs=(vmem, vmem, pl.BlockSpec(memory_space=pltpu.SMEM)),
         scratch_shapes=[
             pltpu.VMEM((4, 2 * rows, width), bf16),
@@ -697,7 +721,8 @@
         + [dma((2, 3)), dma((8,))]
         + [dma((1,))] * 2
         + [dma((8,))] * 2
-        + [dma((blk_count,))] * 2,
+        + [dma((blk_count,))] * 2
+        + [pltpu.VMEM((hard_count, rows), jnp.int32), pltpu.VMEM((1, rows), f32), dma((6,))],
         compiler_params=pltpu.CompilerParams(
             collective_id=0, has_side_effects=True, vmem_limit_bytes=44 * 1024 * 1024
         ),

time: 125 us -> 120 us (0.960)
  Pallas kernels: 116 us -> 111 us
    pallas_call x1, Pallas kernels: 116 us -> 111 us  [on_line(): pl.pallas_call(functools.partial(line_kernel, blk_count), out_shape=(jax....]
where the time goes in v4:
time: 120 us; the launch traced here: 119 us
  Pallas kernels  111 us (92%)
  local copies, waits for them, and re-layouts  6.42 us (5%)
  between operations  2.4 us (2%)
    pallas_call x1, Pallas kernels, on_line(): pl.pallas_call(functools.partial(line_kernel, blk_count), out_shape=(jax....  111 us
    unnamed x10, local copies, waits for them, and re-layouts  6.42 us

profile of v4, /device:TPU:0, one launch (start us, length us, event | category | flops | bytes accessed | tf_op | source)
XLA Modules:
  0.0 119.4 jit_solution(14553976257834559886)
XLA Ops:
  0.6 0.0 copy-start
  0.6 1.2 %copy-done = bf16[128,4096]{1,0:T(8,128)(2,1)S(1)} copy-done((bf16[128,4096]{1,0:T(8,128)(2,1)S(1)}, bf16[128,4096]{1,0:T(8,128)(2,1)}, u32[]{:S(2)}) %copy-start) | copy-done | bytes 1048600
  1.9 0.0 copy-start.1
  1.9 1.2 %copy-done.1 = bf16[128,4096]{1,0:T(8,128)(2,1)S(1)} copy-done((bf16[128,4096]{1,0:T(8,128)(2,1)S(1)}, bf16[128,4096]{1,0:T(8,128)(2,1)}, u32[]{:S(2)}) %copy-start.1) | copy-done | bytes 1048600
  3.1 0.0 copy-start.2
  3.1 0.7 copy-done.2
  3.8 0.0 copy-start.3
  3.8 0.7 copy-done.3
  4.4 110.6 %shard_map.67 = (f32[128,4096]{1,0:T(8,128)S(1)}, f32[128,4096]{1,0:T(8,128)S(1)}, f32[1,1]{1,0:T(1,128)}) custom-call(bf16[128,4096]{1,0:T(8,128)(2,1)S(1)} %copy-done, bf16[128,4096]{1,0:T(8,128)(2,1)S(1)} %copy-done.1, s32[8,128]{1,0:T(8,128)S(1)} %bitcast.3, f32[1,128]{1,0:T(1,128)S(1)} %bitcast.4), custom_call_target="tpu_custom_call" | custom-call | tf_op jit(solution)/shard_map/pallas_call | solution.py:683
  115.1 1.3 %copy.10 = f32[128,4096]{1,0:T(8,128)} copy(f32[128,4096]{1,0:T(8,128)S(1)} %get-tuple-element.12) | data formatting | bytes 4194304
  116.4 1.3 %copy.11 = f32[128,4096]{1,0:T(8,128)} copy(f32[128,4096]{1,0:T(8,128)S(1)} %get-tuple-element.13) | data formatting | bytes 4194304
Async XLA Ops:
  0.6 1.2 %copy-start = (bf16[128,4096]{1,0:T(8,128)(2,1)S(1)}, bf16[128,4096]{1,0:T(8,128)(2,1)}, u32[]{:S(2)}) copy-start(bf16[128,4096]{1,0:T(8,128)(2,1)} %q_ref.1) | copy-start | bytes 3145732
  1.9 1.2 %copy-start.1 = (bf16[128,4096]{1,0:T(8,128)(2,1)S(1)}, bf16[128,4096]{1,0:T(8,128)(2,1)}, u32[]{:S(2)}) copy-start(bf16[128,4096]{1,0:T(8,128)(2,1)} %p_ref.1) | copy-start | bytes 3145732
  3.1 0.7 copy-start.2
  3.8 0.7 copy-start.3

commit v5 on v4

--- a/solution.py
+++ b/solution.py
@@ -68,9 +68,11 @@
 MESH = pl.DeviceIdType.MESH
 HALVES = 2
 CHUNKS = 8
-AHEAD = 3
-FIRST = 3
-LAST = 5
+STEP = CHUNKS // 8
+BEGIN = 2 * STEP
+AHEAD = 3 * STEP
+FIRST = 3 * STEP
+LAST = 5 * STEP
 
 
 def line_kernel(
@@ -337,17 +339,23 @@
         zero = jnp.zeros((rows, 2 * rows), f32)
         lp[zz] = lax.fori_loop(0, width // step, body, zero) * rescale
 
-    def end_logits():
-        @pl.loop(0, 4)
-        def _(zz):
-            def body(k, acc):
-                cols = pl.ds(pl.multiple_of(k * step, step), step)
-                return acc + lax.dot_general(
-                    pq[se, core_rows(c), cols], pp[zz, :, cols], nt, preferred_element_type=f32
-                )
-
-            zero = jnp.zeros((rows, 2 * rows), f32)
-            le[zz] = lax.fori_loop(0, width // step, body, zero) * rescale
+    def end_part(j):
+        cols = pl.ds(j * part, part)
+        left = pq[se, core_rows(c), cols]
+        for zz in (se, sm, mp):
+            term = lax.dot_general(left, pp[zz, :, cols], nt, preferred_element_type=f32)
+            le[zz] = term * rescale if j == 0 else le[zz] + term * rescale
+
+    def both_logits(zz):
+        def body(k, acc):
+            cols = pl.ds(pl.multiple_of(k * step, step), step)
+            left = jnp.concatenate([gq[core_rows(b), cols], pq[se, core_rows(c), cols]], axis=0)
+            return acc + lax.dot_general(left, pp[zz, :, cols], nt, preferred_element_type=f32)
+
+        zero = jnp.zeros((2 * rows, 2 * rows), f32)
+        out = lax.fori_loop(0, width // step, body, zero) * rescale
+        lp[zz] = out[:rows]
+        le[zz] = out[rows:]
 
     def tile_logits():
         def body(k, acc):
@@ -451,6 +459,27 @@
             cols = pl.ds(pl.multiple_of(j * part, part), part)
             pg_ref[:, cols] = jnp.dot(tr[...], gq[:, cols], preferred_element_type=f32)
 
+    def loss_line():
+        for i in range(7):
+            peer = peers[i][1]
+            slot = loss_dp.at[peer]
+            remote(slot, slot, s_ld.at[i], r_ld.at[peer], peers[i]).wait_recv()
+        total = loss_dp[0]
+        for s in range(1, 8):
+            total = total + loss_dp[s]
+        loss_blk[b] = total
+        for i in range(len(others)):
+            lb_copy(i).start()
+
+    def loss_all():
+        for i, other in enumerate(others):
+            slot = loss_blk.at[other]
+            remote(slot, slot, s_lb.at[i], r_lb.at[other], (other, d)).wait_recv()
+        total = loss_blk[0]
+        for g in range(1, blk_count):
+            total = total + loss_blk[g]
+        loss_ref[0, 0] = jnp.max(total) / (rows * blk_count * 8)
+
     @pl.when(z == sm)
     def _():
         for h in range(HALVES):
@@ -486,42 +515,53 @@
         pool_logits(mp)
         group()
         top, total = row_stats()
-        for h in range(HALVES):
+        def take_end(j):
+            wait_q(se, j)
+            q_sib(se, j).start()
+            end_part(j)
+
+        def relay_far(h):
             wait_p(ep, h)
             p_out(ep, h).start()
             p_sib(ep, h).start()
-            if h == 0:
-                q_in(sm, 0, True).start()
-        for j in range(CHUNKS):
-            if 0 < j < AHEAD:
-                q_in(sm, j, True).start()
-            wait_q(se, j)
-            if j < AHEAD:
-                q_in(se, j).start()
-            q_sib(se, j).start()
+
+        relay_far(0)
+        q_in(sm, 0, True).start()
+        for j in range(CHUNKS - STEP):
+            take_end(j)
+        relay_far(1)
+        q_in(se, 0).start()
+        for j in range(1, BEGIN):
+            q_in(sm, j, True).start()
+            q_in(se, j).start()
+        for j in range(CHUNKS - STEP, CHUNKS):
+            take_end(j)
         def q_step(j):
             wait_q(mp, j)
             q_sib(mp, j).start()
             wait_q(ep, j)
             q_sib(ep, j).start()
-            if j + AHEAD < CHUNKS:
+            if j >= STEP and j + AHEAD < CHUNKS:
                 q_in(sm, j + AHEAD, True).start()
                 q_in(se, j + AHEAD).start()
 
         wait_psib(ep)
-        pool_logits(ep)
+        both_logits(ep)
         info = columns_of(d)
         lse, hard = hard_softmax(lp, info, top, total)
         hb[d] = hard.T[0:hard_count, :]
         for n in range(3):
             h_copy(n, d, 0).start()
-        end_logits()
-        q_step(0)
+        for j in range(STEP):
+            q_step(j)
         remote(st_in, st_in, s_st.at[0], r_st.at[0], outer).wait_recv()
         end_hard = hard_softmax(le, columns_of(end_dev), st_in[:, 0:1], st_in[:, 1:2])[1]
         hb[end_dev] = end_hard.T[0:hard_count, :]
         for n in range(3):
             h_copy(n, end_dev, 1).start()
+        for j in range(BEGIN, AHEAD + STEP):
+            q_in(sm, j, True).start()
+            q_in(se, j).start()
 
         def end_grads(j):
             for zz in (se, sm, mp, ep):
@@ -540,12 +580,14 @@
                 acc += jnp.dot(cm[zz], pq[zz, :, cols], preferred_element_type=f32)
             pg_ref[:, cols] = acc
 
-        q_step(1)
+        for j in range(STEP, 2 * STEP):
+            q_step(j)
         query_side(info, lse, hard)
         g_forward(gq, s_gq, r_gq)
-        q_step(2)
+        for j in range(2 * STEP, FIRST):
+            q_step(j)
         query_grads()
-        for j in range(3, CHUNKS):
+        for j in range(FIRST, CHUNKS):
             q_step(j)
             if j == FIRST:
                 for dev in (2 * sm + o, 2 * se + o, 2 * mp, 2 * mp + 1, 2 * ep, 2 * ep + 1):
@@ -562,6 +604,9 @@
                     own_grads(i)
             if j >= LAST:
                 own_grads(j)
+            if j == CHUNKS - 1 - STEP:
+                loss_line()
+        loss_all()
 
         for h in range(HALVES):
             p_in(sm, h, True).wait_send()
@@ -629,7 +674,10 @@
         query_side(info, lse, hard)
         query_grads()
         tile_grads()
+        loss_line()
         for j in range(CHUNKS):
+            if j == CHUNKS - STEP:
+                loss_all()
             cols = pl.ds(j * part, part)
             r_slot = r_in.at[:, cols]
             remote(r_slot, r_slot, s_r.at[j], r_r.at[j], inner).wait_recv()
@@ -642,23 +690,6 @@
         for j in range(CHUNKS):
             q_in(se, j, True).wait_send()
 
-    for i in range(7):
-        peer = peers[i][1]
-        slot = loss_dp.at[peer]
-        remote(slot, slot, s_ld.at[i], r_ld.at[peer], peers[i]).wait_recv()
-    total = loss_dp[0]
-    for s in range(1, 8):
-        total = total + loss_dp[s]
-    loss_blk[b] = total
-    for i in range(len(others)):
-        lb_copy(i).start()
-    for i, other in enumerate(others):
-        slot = loss_blk.at[other]
-        remote(slot, slot, s_lb.at[i], r_lb.at[other], (other, d)).wait_recv()
-    total = loss_blk[0]
-    for g in range(1, blk_count):
-        total = total + loss_blk[g]
-    loss_ref[0, 0] = jnp.max(total) / (rows * blk_count * 8)
     for i in range(len(others)):
         t_copy(i).wait_send()
         lb_copy(i).wait_send()

time: 120 us -> 115 us (0.958)
  Pallas kernels: 111 us -> 106 us
    pallas_call x1, Pallas kernels: 111 us -> 106 us  [on_line(): pl.pallas_call(functools.partial(line_kernel, blk_count), out_shape=(jax....]
where the time goes in v5:
time: 115 us
  Pallas kernels  106 us (92%)
  local copies, waits for them, and re-layouts  6.42 us (6%)
  between operations  2.4 us (2%)
    pallas_call x1, Pallas kernels, on_line(): pl.pallas_call(functools.partial(line_kernel, blk_count), out_shape=(jax....  106 us
    unnamed x10, local copies, waits for them, and re-layouts  6.42 us

profile of v5, /device:TPU:0, one launch (start us, length us, event | category | flops | bytes accessed | tf_op | source)
XLA Modules:
  0.0 115.1 jit_solution(17906967280679870565)
XLA Ops:
  0.6 0.0 copy-start
  0.6 1.2 %copy-done = bf16[128,4096]{1,0:T(8,128)(2,1)S(1)} copy-done((bf16[128,4096]{1,0:T(8,128)(2,1)S(1)}, bf16[128,4096]{1,0:T(8,128)(2,1)}, u32[]{:S(2)}) %copy-start) | copy-done | bytes 1048600
  1.9 0.0 copy-start.1
  1.9 1.2 %copy-done.1 = bf16[128,4096]{1,0:T(8,128)(2,1)S(1)} copy-done((bf16[128,4096]{1,0:T(8,128)(2,1)S(1)}, bf16[128,4096]{1,0:T(8,128)(2,1)}, u32[]{:S(2)}) %copy-start.1) | copy-done | bytes 1048600
  3.1 0.0 copy-start.2
  3.1 0.7 copy-done.2
  3.8 0.0 copy-start.3
  3.8 0.7 copy-done.3
  4.4 106.3 %shard_map.67 = (f32[128,4096]{1,0:T(8,128)S(1)}, f32[128,4096]{1,0:T(8,128)S(1)}, f32[1,1]{1,0:T(1,128)}) custom-call(bf16[128,4096]{1,0:T(8,128)(2,1)S(1)} %copy-done, bf16[128,4096]{1,0:T(8,128)(2,1)S(1)} %copy-done.1, s32[8,128]{1,0:T(8,128)S(1)} %bitcast.3, f32[1,128]{1,0:T(1,128)S(1)} %bitcast.4), custom_call_target="tpu_custom_call" | custom-call | tf_op jit(solution)/shard_map/pallas_call | solution.py:714
  110.7 1.3 %copy.10 = f32[128,4096]{1,0:T(8,128)} copy(f32[128,4096]{1,0:T(8,128)S(1)} %get-tuple-element.12) | data formatting | bytes 4194304
  112.0 1.3 %copy.11 = f32[128,4096]{1,0:T(8,128)} copy(f32[128,4096]{1,0:T(8,128)S(1)} %get-tuple-element.13) | data formatting | bytes 4194304
Async XLA Ops:
  0.6 1.2 %copy-start = (bf16[128,4096]{1,0:T(8,128)(2,1)S(1)}, bf16[128,4096]{1,0:T(8,128)(2,1)}, u32[]{:S(2)}) copy-start(bf16[128,4096]{1,0:T(8,128)(2,1)} %q_ref.1) | copy-start | bytes 3145732
  1.9 1.2 %copy-start.1 = (bf16[128,4096]{1,0:T(8,128)(2,1)S(1)}, bf16[128,4096]{1,0:T(8,128)(2,1)}, u32[]{:S(2)}) copy-start(bf16[128,4096]{1,0:T(8,128)(2,1)} %p_ref.1) | copy-start | bytes 3145732
  3.1 0.7 copy-start.2
  3.8 0.7 copy-start.3
